TPU v7x, 256 devices: a whole 4x4x8 slice. The times are simulated.
256 devices in a mesh: path: 16 (over z, core), col: 16 (over y, x).
Axes of the slice: x: 4, y: 4, z: 8, core: 2. Of those that a mesh axis runs over, the one named last changes fastest.
Arguments:
- exposure: bfloat16 [65536, 16384], P('path', 'col'), may hold values from -127 to 127
- scales: float32 [128, 65536], P('col', 'path'), may hold values from 0.003 to 0.27, as said below
- sketch: bfloat16 [32, 16384], P(None, 'col'), may hold values from -0.046875 to 0.046875
Outputs:
- basis: float32 [32, 65536], P(None, 'path')
- projected: float32 [32, 16384], P(None, 'col')
Inputs may be any that keep to these rules, and one draw needn't show every extreme that they name: `scales`: positive.
All inputs are finite; a program needn't handle non-finite values.
Results may differ from a plain program's by a relative error of at most 0.0003.
Values sent between devices are 32-bit elements; how exact they have to be, the bound alone decides.
No kernel may reach another device: no remote copies, remote signals or barrier semaphores. Data moves between devices by JAX's collectives and lax.ppermute only.
A program may use at most 64 MiB of HBM per device.

v0:
```python
import jax
import jax.numpy as jnp
from jax import lax
from jax.sharding import PartitionSpec as P

HIGH = lax.Precision.HIGHEST


def per_device(exposure, scales, sketch):
    row_count = exposure.shape[0]
    block_count = scales.shape[0]
    codes = exposure.reshape(row_count, block_count, 128)
    sketch3 = sketch.reshape(sketch.shape[0], block_count, 128)
    parts = lax.dot_general(
        sketch3, codes, (((2,), (2,)), ((1,), (1,))), preferred_element_type=jnp.float32
    )
    partial_value = jnp.sum(parts * scales[:, None, :], axis=0)
    sketched = lax.psum(partial_value, "col")
    gram_total = lax.psum(jnp.dot(sketched, sketched.T, precision=HIGH), "path")
    factor = jnp.linalg.cholesky(gram_total)
    orthonormal = lax.linalg.triangular_solve(factor, sketched, left_side=True, lower=True)
    weighted = orthonormal[None, :, :] * scales[:, None, :]
    term = lax.dot_general(
        weighted, codes.astype(jnp.float32), (((2,), (0,)), ((0,), (1,))), precision=HIGH
    )
    local_proj = term.transpose(1, 0, 2).reshape(orthonormal.shape[0], block_count * 128)
    projected = lax.psum(local_proj, "path")
    total_paths = row_count * lax.axis_size("path")
    basis = orthonormal * jnp.sqrt(jnp.float32(total_paths))
    return (basis, projected)


def solution(mesh):
    placed = (P("path", "col"), P("col", "path"), P(None, "col"))
    return jax.shard_map(
        per_device,
        mesh=mesh,
        in_specs=placed,
        out_specs=(P(None, "path"), P(None, "col")),
        check_vma=False,
    )
```

profile of v0, /device:TPU:1, one launch (start us, length us, event | category | flops | bytes accessed | tf_op | source)
XLA Modules:
  0.0 293.7 jit_solution(8979144331565636396)
XLA Ops:
  7.2 0.0 copy-start
  7.2 0.0 copy-start.1
  7.2 0.0 all-reduce.3.cloned.1.call-start
  7.2 0.8 copy-done
  8.0 7.3 %fusion.12 = f32[32,4096]{1,0:T(8,128)} fusion(f32[8,4096]{1,0:T(8,128)} %param.4, bf16[4096,1024]{1,0:T(8,128)(2,1)} %param.3, bf16[32,1024]{1,0:T(8,128)(2,1)S(1)} %copy-done), kind=kOutput, calls=%fused_computation.10 | convolution fusion | flops 270401536 | bytes 9109504 | tf_op jit(solution)/shard_map/dot_general | solution.py:14
  15.3 0.0 all-reduce.3.cloned.1.call-update
  15.3 0.0 all-reduce.5.cloned.1.call-start
  15.3 97.9 %all-reduce.3.cloned.1.call-done = f32[32,4096]{1,0:T(8,128)} async-done(((f32[32,4096]{1,0:T(8,128)}), f32[32,4096]{1,0:T(8,128)}) %all-reduce.3.cloned.1.call-update) | async-done | bytes 524304 | tf_op jit(solution)/shard_map/psum | solution.py:18
  113.2 1.8 fusion.26
  115.0 45.4 %psum.22 = f32[32,32]{0,1:T(8,128)S(1)} all-reduce(f32[32,32]{0,1:T(8,128)S(1)} %fusion.26), channel_id=1, replica_groups=mesh['path'=16,'col'=16] {'path'}, use_global_device_ids=true, to_apply=%region_2.0 | all-reduce | flops 1024 | bytes 8192 | tf_op jit(solution)/shard_map/psum | solution.py:19
  160.4 0.1 copy.13
  160.5 2.9 cholesky.16
  163.5 0.6 compare_reduce_fusion
  164.1 0.7 fusion.22
  164.8 2.4 custom-call.6
  167.2 2.5 broadcast_multiply_fusion
  169.7 0.0 copy-done.1
  169.7 6.3 %fusion.15 = f32[8,4,8,128]{3,2,1,0:T(8,128)S(1)} fusion(f32[32,4096]{1,0:T(8,128)S(1)} %get-tuple-element.3, f32[8,4096]{1,0:T(8,128)S(1)} %copy-done.1, bf16[4096,1024]{1,0:T(8,128)(2,1)} %param.3), kind=kOutput, calls=%fused_computation.11 | convolution fusion | flops 1611661312 | bytes 9175040 | tf_op jit(solution)/shard_map/dot_general | solution.py:23
  176.0 0.7 copy.39
  176.7 0.0 all-reduce.5.cloned.1.call-update
  176.7 108.7 %all-reduce.5.cloned.1.call-done = f32[32,1024]{1,0:T(8,128)} async-done(((f32[32,1024]{1,0:T(8,128)}), f32[32,1024]{1,0:T(8,128)}) %all-reduce.5.cloned.1.call-update) | async-done | bytes 131088 | tf_op jit(solution)/shard_map/psum | solution.py:27
  285.3 1.6 copy.42
  (2 shorter events, 0.0 us)
Async XLA Ops:
  7.2 0.8 copy-start
  7.2 162.5 %copy-start.1 = (f32[8,4096]{1,0:T(8,128)S(1)}, f32[8,4096]{1,0:T(8,128)}, u32[]{:S(2)}) copy-start(f32[8,4096]{1,0:T(8,128)} %param.4) | copy-start | bytes 393220
  7.2 106.0 %all-reduce.3.cloned.1.call-start = ((), (), s32[]{:S(2)}) async-start(), calls=%async_computation | async-start | bytes 1048576 | tf_op jit(solution)/shard_map/psum | solution.py:18
  15.3 270.1 %all-reduce.5.cloned.1.call-start = ((), (), s32[]{:S(2)}) async-start(), calls=%async_computation.1 | async-start | bytes 262144 | tf_op jit(solution)/shard_map/psum | solution.py:27
Sparse Core Ops, SparseCore 0:
  15.4 97.7 all-reduce.2
  176.8 108.4 all-reduce.4
where the time goes:
time: 294 us
  waiting for transfers between devices  207 us (70%)
  blocking collectives  45.4 us (15%)
  matrix products  17.8 us (6%)
  between operations  14.1 us (5%)
  other arithmetic  6.69 us (2%)
  local copies, waits for them, and re-layouts  3.09 us (1%)
    psum x1, waiting for transfers between devices, per_device(): projected = lax.psum(local_proj, 'path')  109 us
    psum x1, waiting for transfers between devices, per_device(): sketched = lax.psum(partial_value, 'col')  97.9 us
    psum x1, blocking collectives, per_device(): gram_total = lax.psum(jnp.dot(sketched, sketched.T, precision=HIGH), 'path')  45.4 us
    dot_general x1, matrix products, per_device(): lax.dot_general(sketch3, codes, (((2,), (2,)), ((1,), (1,))), preferred_e...  7.25 us
    dot_general x1, matrix products, per_device(): lax.dot_general(weighted, codes.astype(jnp.float32), (((2,), (0,)), ((0,)...  6.3 us
  transfers between devices with their start and end apart: 2, of which 2 were waited for; matrix products, arithmetic and copies ran while one was open for 0% of the time, Pallas kernels for 0%

commit v1 on v0

v1 whole, which is shorter than its diff:
```python
import functools
import jax
import jax.numpy as jnp
from jax import lax
from jax.experimental import pallas as pl
from jax.experimental.pallas import tpu as pltpu
from jax.sharding import PartitionSpec as P

BF = jnp.bfloat16
F32 = jnp.float32
ANY = pl.BlockSpec(memory_space=pl.ANY)
VM = pl.BlockSpec(memory_space=pltpu.VMEM)
LIMIT = 40 * 1024 * 1024
CHUNKS = 4
NT = (((1,), (1,)), ((), ()))


def split2(x):
    hi = x.astype(BF)
    return hi, (x - hi.astype(F32)).astype(BF)


def sketch_kernel(groups, sketch, scales, exposure, out, kept, sems):
    rows, cols = exposure.shape
    blocks = scales.shape[0]
    width = out.shape[2]
    step = rows // CHUNKS
    copies = []
    for c in range(CHUNKS):
        part = pl.ds(c * step, step)
        copies.append(pltpu.make_async_copy(exposure.at[part], kept.at[part], sems.at[c]))
        copies[-1].start()
    for c in range(CHUNKS):
        copies[c].wait()

        @pl.loop(0, step // width)
        def _(i):
            start = pl.multiple_of(c * step + i * width, width)
            span = pl.ds(start, width)
            total = None
            for b in range(blocks):
                lanes = slice(b * 128, (b + 1) * 128)
                term = lax.dot_general(
                    sketch[:, lanes], kept[span, lanes], NT, preferred_element_type=F32
                )
                term = term * scales[b : b + 1, span]
                total = term if total is None else total + term
            out[c * (step // width) + i] = total


def sum_copies_kernel(x, out):
    total = jnp.sum(x[...], axis=0)
    for j in range(out.shape[0]):
        out[j] = total


def add_copies_kernel(a, b, out):
    total = a[...] + b[...]
    for j in range(out.shape[0]):
        out[j] = total


def project_kernel(core, pieces, scales, exposure, mine, other, acc, gram):
    groups, size, width = pieces.shape
    blocks = scales.shape[0]
    acc[...] = jnp.zeros_like(acc)
    gram[...] = jnp.zeros_like(gram)

    @pl.loop(0, groups)
    def _(g):
        span = pl.ds(pl.multiple_of(g * width, width), width)
        s = pieces[g]
        both = jnp.concatenate(split2(s), axis=0)
        gram[...] += lax.dot_general(both, both, NT, preferred_element_type=F32)
        for b in range(blocks):
            lanes = slice(b * 128, (b + 1) * 128)
            w = jnp.concatenate(split2(s * scales[b : b + 1, span]), axis=0)
            acc[:, lanes] += jnp.dot(w, exposure[span, lanes], preferred_element_type=F32)

    half = blocks * 128 // 2
    first = core[0] == 0
    low = acc[:size, :half] + acc[size:, :half]
    high = acc[:size, half:] + acc[size:, half:]
    g = gram[...]
    g = (g[:size, :size] + g[size:, size:]) + (g[:size, size:] + g[size:, :size])
    for ref, part in ((mine, jnp.where(first, low, high)), (other, jnp.where(first, high, low))):
        ref[:, :half] = part
        ref[:, half:] = jnp.zeros_like(ref[:, half:])
        ref[:, half : half + size] = g


def solve_kernel(x, lower, projected):
    size = x.shape[1]
    half = projected.shape[1]
    total = jnp.sum(x[...], axis=0)
    gram = total[:, half : half + size]
    row = lax.broadcasted_iota(jnp.int32, (size, 128), 0)
    lane = lax.broadcasted_iota(jnp.int32, (size, 128), 1)
    eye = jnp.where(lane - size == row, 1.0, 0.0).astype(F32)
    a = jnp.where(lane < size, jnp.pad(gram, ((0, 0), (0, 128 - size))), eye)
    inv = jnp.zeros((size, 128), F32)
    for j in range(size):
        pivot_row = a[j : j + 1, :]
        pivot = pivot_row[:, j : j + 1]
        root = lax.rsqrt(pivot)
        inv = jnp.where(row == j, pivot_row * root, inv)
        if j < size - 1:
            col = a[:, j : j + 1]
            a = a - jnp.where(row > j, (col / pivot) * pivot_row, 0.0)
    linv = inv[:, size : 2 * size]
    lower[...] = linv
    projected[...] = lax.dot_general(
        linv, total[:, :half], (((1,), (0,)), ((), ())),
        precision=lax.Precision.HIGHEST, preferred_element_type=F32,
    )


def basis_kernel(factor, lower, pieces, out):
    groups, size, width = pieces.shape
    hi, lo = split2(lower[...] * factor)
    lhs = jnp.concatenate([hi, lo, hi, lo], axis=1)
    for g in range(groups):
        shi, slo = split2(pieces[g])
        rhs = jnp.concatenate([shi, shi, slo, slo], axis=0)
        out[:, g * width : (g + 1) * width] = jnp.dot(lhs, rhs, preferred_element_type=F32)


def join_kernel(core, mine, other, out):
    half = mine.shape[1]
    first = core[0] == 0
    a, b = mine[...], other[...]
    out[:, :half] = jnp.where(first, a, b)
    out[:, half:] = jnp.where(first, b, a)


def params(**kw):
    return pltpu.CompilerParams(vmem_limit_bytes=LIMIT, **kw)


def per_device(exposure, scales, sketch):
    rows, cols = exposure.shape
    size = sketch.shape[0]
    blocks = scales.shape[0]
    n_col = lax.axis_size(("y", "x"))
    n_z = lax.axis_size("z")
    width = rows // n_col
    half = cols // 2
    wide = half + 128
    total_paths = rows * n_z * lax.axis_size("core")
    core = lax.axis_index("core").astype(jnp.int32).reshape(1)
    SM = pl.BlockSpec(memory_space=pltpu.SMEM)
    shape = jax.ShapeDtypeStruct

    partial, kept = pl.pallas_call(
        functools.partial(sketch_kernel, n_col),
        out_shape=(shape((n_col, size, width), F32), pltpu.VMEM((rows, cols), BF)),
        in_specs=[VM, VM, ANY],
        out_specs=(VM, VM),
        scratch_shapes=[pltpu.SemaphoreType.DMA((CHUNKS,))],
        compiler_params=params(),
        name="sketch",
    )(sketch, scales, exposure)

    got = lax.all_to_all(partial, ("y", "x"), 0, 0)
    spread = pl.pallas_call(
        sum_copies_kernel, out_shape=shape((n_col, size, width), F32),
        in_specs=[VM], out_specs=VM, compiler_params=params(), name="sum_parts",
    )(got)
    pieces = lax.all_to_all(spread, ("y", "x"), 0, 0)

    kept = pltpu.with_memory_space_constraint(kept, pltpu.VMEM)
    mine, other = pl.pallas_call(
        project_kernel,
        out_shape=(shape((size, wide), F32),) * 2,
        in_specs=[SM, VM, VM, VM],
        out_specs=(VM, VM),
        scratch_shapes=[pltpu.VMEM((2 * size, cols), F32), pltpu.VMEM((2 * size, 2 * size), F32)],
        compiler_params=params(),
        name="project",
    )(core, pieces, scales, kept)

    received = lax.ppermute(other, "core", [(0, 1), (1, 0)])
    spread_z = pl.pallas_call(
        add_copies_kernel, out_shape=shape((n_z, size, wide), F32),
        in_specs=[VM, VM], out_specs=VM, compiler_params=params(), name="add_cores",
    )(mine, received)
    got_z = lax.all_to_all(spread_z, "z", 0, 0)

    lower, proj = pl.pallas_call(
        solve_kernel, out_shape=(shape((size, size), F32), shape((size, half), F32)),
        in_specs=[VM], out_specs=(VM, VM), compiler_params=params(), name="solve",
    )(got_z)
    proj_other = lax.ppermute(proj, "core", [(0, 1), (1, 0)])
    basis = pl.pallas_call(
        functools.partial(basis_kernel, float(total_paths) ** 0.5),
        out_shape=shape((size, rows), F32),
        in_specs=[VM, VM], out_specs=VM, compiler_params=params(), name="basis",
    )(lower, pieces)
    projected = pl.pallas_call(
        join_kernel, out_shape=shape((size, cols), F32),
        in_specs=[SM, VM, VM], out_specs=VM, compiler_params=params(), name="join",
    )(core, proj, proj_other)
    return (basis, projected)


def solution(mesh):
    path, col = ("z", "core"), ("y", "x")
    n_path, n_col = mesh.shape["path"], mesh.shape["col"]
    split = jax.sharding.Mesh(mesh.devices.reshape(n_path // 2, 2, 4, n_col // 4), path + col)
    return jax.shard_map(
        per_device,
        mesh=split,
        in_specs=(P(path, col), P(col, path), P(None, col)),
        out_specs=(P(None, path), P(None, col)),
        check_vma=False,
    )
```

time: 294 us -> 89.2 us (0.30)
  waiting for transfers between devices: 207 us -> 10.6 us
  matrix products: 17.8 us -> 0 us
  Pallas kernels: 0 us -> 15.7 us
  between operations: 14.1 us -> 0.68 us
  starting transfers between devices: 0.08 us -> 8.16 us
  other arithmetic: 6.69 us -> 0 us
  local copies, waits for them, and re-layouts: 3.09 us -> 8.33 us
    psum x2 -> x0, waiting for transfers between devices: 207 us -> none  [the longest x1 109 us: per_device(): projected = lax.psum(local_proj, 'path')]
    psum x1 -> x0, blocking collectives: 45.4 us -> none  [per_device(): gram_total = lax.psum(jnp.dot(sketched, sketched.T, precision=HIGH), 'path')]
    all_to_all x0 -> x2, blocking collectives: none -> 45.4 us  [the longest x1 27.6 us: per_device(): got_z = lax.all_to_all(spread_z, 'z', 0, 0)]
    pallas_call x0 -> x7, Pallas kernels: none -> 15.7 us  [the longest x1 6.24 us: per_device(): pl.pallas_call(functools.partial(sketch_kernel, n_col), out_shape=(shape(...]
    dot_general x3 -> x0, matrix products: 15.3 us -> none  [the longest x1 7.25 us: per_device(): lax.dot_general(sketch3, codes, (((2,), (2,)), ((1,), (1,))), preferred_e...]
    all_to_all x0 -> x1, waiting for transfers between devices: none -> 9.65 us  [per_device(): pieces = lax.all_to_all(spread, ('y', 'x'), 0, 0)]
    another operation x5 -> x0, other arithmetic: 6.68 us -> none  [the longest x3 3.59 us: per_device(): factor = jnp.linalg.cholesky(gram_total)]
    unnamed x5 -> x10, local copies, waits for them, and re-layouts: 2.35 us -> 8.33 us
  transfers between devices with their start and end apart: 2 -> 3, of which waited for: 2 -> 2; matrix products, arithmetic and copies ran while one was open for 0% -> 0% of each run, Pallas kernels for 0% -> 1%
where the time goes in v1:
time: 89.2 us; the launch traced here: 88.9 us
  blocking collectives  45.4 us (51%)
  Pallas kernels  15.7 us (18%)
  waiting for transfers between devices  10.6 us (12%)
  local copies, waits for them, and re-layouts  8.33 us (9%)
  starting transfers between devices  8.16 us (9%)
    all_to_all x1, blocking collectives, per_device(): got_z = lax.all_to_all(spread_z, 'z', 0, 0)  27.6 us
    all_to_all x1, blocking collectives, per_device(): got = lax.all_to_all(partial, ('y', 'x'), 0, 0)  17.9 us
    all_to_all x1, waiting for transfers between devices, per_device(): pieces = lax.all_to_all(spread, ('y', 'x'), 0, 0)  9.65 us
    unnamed x10, local copies, waits for them, and re-layouts  8.33 us
    pallas_call x1, Pallas kernels, per_device(): pl.pallas_call(functools.partial(sketch_kernel, n_col), out_shape=(shape(...  6.24 us
    pallas_call x1, Pallas kernels, per_device(): pl.pallas_call(project_kernel, out_shape=(shape((size, wide), F32),) * 2,...  3.92 us
    all_to_all x1, starting transfers between devices, per_device(): pieces = lax.all_to_all(spread, ('y', 'x'), 0, 0)  3.57 us
    ppermute x1, starting transfers between devices, per_device(): received = lax.ppermute(other, 'core', [(0, 1), (1, 0)])  2.87 us
  transfers between devices with their start and end apart: 3, of which 2 were waited for; matrix products, arithmetic and copies ran while one was open for 0% of the time, Pallas kernels for 1%

profile of v1, /device:TPU:1, one launch (start us, length us, event | category | flops | bytes accessed | tf_op | source)
XLA Modules:
  0.0 88.9 jit_solution(9857958705322406767)
XLA Ops:
  0.6 0.0 copy-start.2
  0.6 0.9 %copy-done.2 = f32[8,4096]{1,0:T(8,128)S(1)} copy-done((f32[8,4096]{1,0:T(8,128)S(1)}, f32[8,4096]{1,0:T(8,128)}, u32[]{:S(2)}) %copy-start.2) | copy-done | bytes 131096
  1.5 0.0 copy-start.4
  1.5 0.8 copy-done.4
  2.4 0.0 copy-start.3
  2.4 6.2 %sketch.2 = (f32[16,32,256]{2,1,0:T(8,128)S(1)}, bf16[4096,1024]{1,0:T(8,128)(2,1)S(1)}) custom-call(bf16[32,1024]{1,0:T(8,128)(2,1)S(1)} %copy-done.4, f32[8,4096]{1,0:T(8,128)S(1)} %copy-done.2, bf16[4096,1024]{1,0:T(8,128)(2,1)} %exposure.1), custom_call_target="tpu_custom_call" | custom-call | tf_op jit(solution)/shard_map/sketch/pallas_call | solution.py:154
  8.6 0.0 copy-start
  8.6 3.2 %copy-done = bf16[4096,1024]{1,0:T(8,128)(2,1)} copy-done((bf16[4096,1024]{1,0:T(8,128)(2,1)}, bf16[4096,1024]{1,0:T(8,128)(2,1)S(1)}, u32[]{:S(2)}) %copy-start) | copy-done | bytes 8388632
  11.8 17.9 %all_to_all.15.x = f32[16,32,256]{2,1,0:T(8,128)S(1)} all-to-all(f32[16,32,256]{2,1,0:T(8,128)S(1)} %get-tuple-element.8), channel_id=1, replica_groups=mesh['z'=8,'core'=2,'y'=4,'x'=4] {'y','x'}, dimensions={0} | all-to-all | bytes 1048576 | tf_op jit(solution)/shard_map/all_to_all | solution.py:164
  29.7 0.9 sum_parts.1
  30.6 3.6 %all-to-all-start.1 = ((f32[16,32,256]{2,1,0:T(8,128)}), f32[16,32,256]{2,1,0:T(8,128)S(1)}, u32[]{:S(2)}, u32[]{:S(2)}) async-start(f32[16,32,256]{2,1,0:T(8,128)} %sum_parts.1), calls=%async_computation.1 | async-start | bytes 1048576 | tf_op jit(solution)/shard_map/all_to_all | solution.py:169
  34.2 9.7 %all-to-all-done.1.pieces = f32[16,32,256]{2,1,0:T(8,128)S(1)} async-done(((f32[16,32,256]{2,1,0:T(8,128)}), f32[16,32,256]{2,1,0:T(8,128)S(1)}, u32[]{:S(2)}, u32[]{:S(2)}) %all-to-all-start.1) | async-done | bytes 524320 | tf_op jit(solution)/shard_map/all_to_all | solution.py:169
  43.8 0.0 copy-done.3
  43.8 0.0 copy-start.1
  43.8 3.4 %copy-done.1 = bf16[4096,1024]{1,0:T(8,128)(2,1)S(1)} copy-done((bf16[4096,1024]{1,0:T(8,128)(2,1)S(1)}, bf16[4096,1024]{1,0:T(8,128)(2,1)}, u32[]{:S(2)}) %copy-start.1) | copy-done | bytes 8388632
  47.2 3.9 %project.1 = (f32[32,640]{1,0:T(8,128)S(1)}, f32[32,640]{1,0:T(8,128)S(1)}) custom-call(s32[1]{0:T(128)} %bitcast.core, f32[16,32,256]{2,1,0:T(8,128)S(1)} %all-to-all-done.1.pieces, f32[8,4096]{1,0:T(8,128)S(1)} %copy-done.3, bf16[4096,1024]{1,0:T(8,128)(2,1)S(1)} %copy-done.1), custom_call_target="tpu_custom_call" | custom-call | tf_op jit(solution)/shard_map/project/pallas_call | solution.py:172
  51.1 2.9 %collective-permute-start = (f32[32,640]{1,0:T(8,128)S(1)}, f32[32,640]{1,0:T(8,128)S(1)}, u32[]{:S(2)}, u32[]{:S(2)}) collective-permute-start(f32[32,640]{1,0:T(8,128)S(1)} %get-tuple-element.11), channel_id=1, source_target_pairs={{0,16},{16,0},{1,17},{17,1},{2,18},{18,2},{3,19},{19,3},{4,20},{20... | collective-permute-start | bytes 245768 | tf_op jit(solution)/shard_map/ppermute | solution.py:182
  54.0 0.9 %collective-permute-done.b = f32[32,640]{1,0:T(8,128)S(1)} collective-permute-done((f32[32,640]{1,0:T(8,128)S(1)}, f32[32,640]{1,0:T(8,128)S(1)}, u32[]{:S(2)}, u32[]{:S(2)}) %collective-permute-start) | collective-permute-done | bytes 81952 | tf_op jit(solution)/shard_map/ppermute | solution.py:182
  55.0 27.6 %all_to_all.16.x = f32[8,32,640]{2,1,0:T(8,128)S(1)} all-to-all(f32[8,32,640]{2,1,0:T(8,128)S(1)} %add_cores.1), channel_id=1, replica_groups=mesh['z'=8,'core'=2,'y'=4,'x'=4] {'z'}, dimensions={0} | all-to-all | bytes 1310720 | tf_op jit(solution)/shard_map/all_to_all | solution.py:187
  82.5 2.8 %solve.1 = (f32[32,32]{1,0:T(8,128)S(1)}, f32[32,512]{1,0:T(8,128)S(1)}) custom-call(f32[8,32,640]{2,1,0:T(8,128)S(1)} %all_to_all.16.x), custom_call_target="tpu_custom_call" | custom-call | tf_op jit(solution)/shard_map/solve/pallas_call | solution.py:189
  85.4 1.7 %collective-permute-start.1 = (f32[32,512]{1,0:T(8,128)S(1)}, f32[32,512]{1,0:T(8,128)S(1)}, u32[]{:S(2)}, u32[]{:S(2)}) collective-permute-start(f32[32,512]{1,0:T(8,128)S(1)} %get-tuple-element.13.mine), channel_id=1, source_target_pairs={{0,16},{16,0},{1,17},{17,1},{2,18},{18,2},{3,19},{19,3},{4,20},{20... | collective-permute-start | bytes 196616 | tf_op jit(solution)/shard_map/ppermute | solution.py:193
  87.1 1.1 %basis.1 = f32[32,4096]{1,0:T(8,128)} custom-call(f32[32,32]{1,0:T(8,128)S(1)} %get-tuple-element.12.lower, f32[16,32,256]{2,1,0:T(8,128)S(1)} %all-to-all-done.1.pieces), custom_call_target="tpu_custom_call" | custom-call | tf_op jit(solution)/shard_map/basis/pallas_call | solution.py:194
  88.2 0.0 collective-permute-done.1.other
  88.2 0.7 join.1
  (1 shorter events, 0.0 us)
Async XLA Ops:
  0.6 0.9 %copy-start.2 = (f32[8,4096]{1,0:T(8,128)S(1)}, f32[8,4096]{1,0:T(8,128)}, u32[]{:S(2)}) copy-start(f32[8,4096]{1,0:T(8,128)} %scales.3) | copy-start | bytes 393220
  1.5 0.8 copy-start.4
  2.4 41.5 %copy-start.3 = (f32[8,4096]{1,0:T(8,128)S(1)}, f32[8,4096]{1,0:T(8,128)}, u32[]{:S(2)}) copy-start(f32[8,4096]{1,0:T(8,128)} %scales.3) | copy-start | bytes 393220
  8.6 3.2 %copy-start = (bf16[4096,1024]{1,0:T(8,128)(2,1)}, bf16[4096,1024]{1,0:T(8,128)(2,1)S(1)}, u32[]{:S(2)}) copy-start(bf16[4096,1024]{1,0:T(8,128)(2,1)S(1)} %get-tuple-element.9.exposure) | copy-start | bytes 25165828
  30.6 13.2 %all-to-all-start.1 = ((f32[16,32,256]{2,1,0:T(8,128)}), f32[16,32,256]{2,1,0:T(8,128)S(1)}, u32[]{:S(2)}, u32[]{:S(2)}) async-start(f32[16,32,256]{2,1,0:T(8,128)} %sum_parts.1), calls=%async_computation.1 | async-start | bytes 1048576 | tf_op jit(solution)/shard_map/all_to_all | solution.py:169
  43.8 3.4 %copy-start.1 = (bf16[4096,1024]{1,0:T(8,128)(2,1)S(1)}, bf16[4096,1024]{1,0:T(8,128)(2,1)}, u32[]{:S(2)}) copy-start(bf16[4096,1024]{1,0:T(8,128)(2,1)} %copy-done) | copy-start | bytes 25165828
  51.1 3.8 %collective-permute-start = (f32[32,640]{1,0:T(8,128)S(1)}, f32[32,640]{1,0:T(8,128)S(1)}, u32[]{:S(2)}, u32[]{:S(2)}) collective-permute-start(f32[32,640]{1,0:T(8,128)S(1)} %get-tuple-element.11), channel_id=1, source_target_pairs={{0,16},{16,0},{1,17},{17,1},{2,18},{18,2},{3,19},{19,3},{4,20},{20... | collective-permute-start | bytes 245768 | tf_op jit(solution)/shard_map/ppermute | solution.py:182
  85.4 2.8 %collective-permute-start.1 = (f32[32,512]{1,0:T(8,128)S(1)}, f32[32,512]{1,0:T(8,128)S(1)}, u32[]{:S(2)}, u32[]{:S(2)}) collective-permute-start(f32[32,512]{1,0:T(8,128)S(1)} %get-tuple-element.13.mine), channel_id=1, source_target_pairs={{0,16},{16,0},{1,17},{17,1},{2,18},{18,2},{3,19},{19,3},{4,20},{20... | collective-permute-start | bytes 196616 | tf_op jit(solution)/shard_map/ppermute | solution.py:193

commit v2 on v0

v2 whole, which is shorter than its diff:
```python
import functools
import jax
import jax.numpy as jnp
from jax import lax
from jax.experimental import pallas as pl
from jax.experimental.pallas import tpu as pltpu
from jax.sharding import PartitionSpec as P

BF = jnp.bfloat16
F32 = jnp.float32
ANY = pl.BlockSpec(memory_space=pl.ANY)
VM = pl.BlockSpec(memory_space=pltpu.VMEM)
SM = pl.BlockSpec(memory_space=pltpu.SMEM)
CHUNKS = 4
LANES = 128
NT = (((1,), (1,)), ((), ()))


def split2(x):
    hi = x.astype(BF)
    return hi, (x - hi.astype(F32)).astype(BF)


def lanes(b, n=1):
    return slice(b * LANES, (b + n) * LANES)


def fetch(exposure, held, sems):
    step = held.shape[0] // CHUNKS
    copies = []
    for c in range(CHUNKS):
        part = pl.ds(c * step, step)
        copies.append(pltpu.make_async_copy(exposure.at[part], held.at[part], sems.at[c]))
        copies[-1].start()
    return copies


def sketch_kernel(sketch_hbm, scales_hbm, exposure, out, sketch, scales, held, diag, sems, small):
    size = sketch.shape[0]
    blocks = scales.shape[0]
    groups, _, width = out.shape
    per_chunk = groups // CHUNKS
    first = pltpu.make_async_copy(sketch_hbm, sketch, small.at[0])
    second = pltpu.make_async_copy(scales_hbm, scales, small.at[1])
    first.start()
    second.start()
    copies = fetch(exposure, held, sems)
    diag[...] = jnp.zeros_like(diag)
    first.wait()
    for b in range(blocks):
        diag[b * size : (b + 1) * size, lanes(b)] = sketch[:, lanes(b)]
    second.wait()
    for c in range(CHUNKS):
        copies[c].wait()
        for g in range(c * per_chunk, (c + 1) * per_chunk):
            span = slice(g * width, (g + 1) * width)
            parts = lax.dot_general(diag[...], held[span, :], NT, preferred_element_type=F32)
            total = None
            for b in range(blocks):
                term = parts[b * size : (b + 1) * size] * scales[b : b + 1, span]
                total = term if total is None else total + term
            out[g] = total


def sum_copies_kernel(x, out):
    total = jnp.sum(x[...], axis=0)
    for j in range(out.shape[0]):
        out[j] = total


def add_copies_kernel(a, b, out):
    total = a[...] + b[...]
    for j in range(out.shape[0]):
        out[j] = total


def sum_kernel(x, out):
    out[...] = jnp.sum(x[...], axis=0)


def project_kernel(core, pieces, scales_hbm, exposure, mine, other, scales, held, both, w, acc, sems, small):
    groups, size, width = pieces.shape
    blocks = scales.shape[0]
    per_chunk = groups // CHUNKS
    step = held.shape[0] // CHUNKS
    first = pltpu.make_async_copy(scales_hbm, scales, small.at[0])
    first.start()
    copies = fetch(exposure, held, sems)
    for g in range(groups):
        both[:, g * width : (g + 1) * width] = jnp.concatenate(split2(pieces[g]), axis=0)
    gram = lax.dot_general(both[...], both[...], NT, preferred_element_type=F32)
    gram = (gram[:size, :size] + gram[size:, size:]) + (gram[:size, size:] + gram[size:, :size])
    first.wait()
    for c in range(CHUNKS):
        for g in range(c * per_chunk, (c + 1) * per_chunk):
            span = slice(g * width, (g + 1) * width)
            s = pieces[g]
            for b in range(blocks):
                w[2 * size * b : 2 * size * (b + 1), span] = jnp.concatenate(
                    split2(s * scales[b : b + 1, span]), axis=0
                )
        copies[c].wait()
        rows = slice(c * step, (c + 1) * step)
        for b in range(0, blocks, 2):
            t = jnp.dot(
                w[2 * size * b : 2 * size * (b + 2), rows], held[rows, lanes(b, 2)],
                preferred_element_type=F32,
            )
            t0 = t[:size, :LANES] + t[size : 2 * size, :LANES]
            t1 = t[2 * size : 3 * size, LANES:] + t[3 * size :, LANES:]
            if c == 0:
                acc[b] = t0
                acc[b + 1] = t1
            else:
                acc[b] += t0
                acc[b + 1] += t1

    half = blocks // 2
    is_first = core[0] == 0
    for b in range(half):
        low, high = acc[b], acc[half + b]
        mine[b * size : (b + 1) * size] = jnp.where(is_first, low, high)
        other[b * size : (b + 1) * size] = jnp.where(is_first, high, low)
    rows = LANES // size
    packed = jnp.concatenate([gram[i * size // rows : (i + 1) * size // rows] for i in range(rows)], axis=1)
    mine[half * size :] = packed
    other[half * size :] = packed


def solve_kernel(factor, x, pieces, lower, basis):
    groups, size, width = pieces.shape
    rows = LANES // size
    packed = x[x.shape[0] - size // rows :, :]
    gram = jnp.concatenate([packed[:, i * size : (i + 1) * size] for i in range(rows)], axis=0)
    row = lax.broadcasted_iota(jnp.int32, (size, LANES), 0)
    lane = lax.broadcasted_iota(jnp.int32, (size, LANES), 1)
    eye = jnp.where(lane - size == row, 1.0, 0.0).astype(F32)
    a = jnp.where(lane < size, jnp.pad(gram, ((0, 0), (0, LANES - size))), eye)
    inv = jnp.zeros((size, LANES), F32)
    for j in range(size):
        pivot_row = a[j : j + 1, :]
        pivot = pivot_row[:, j : j + 1]
        inv = jnp.where(row == j, pivot_row * lax.rsqrt(pivot), inv)
        if j < size - 1:
            col = a[:, j : j + 1]
            a = a - jnp.where(row > j, (col / pivot) * pivot_row, 0.0)
    linv = inv[:, size : 2 * size]
    lower[...] = linv
    hi, lo = split2(linv * factor)
    lhs = jnp.concatenate([hi, lo, hi, lo], axis=1)
    for g in range(groups):
        shi, slo = split2(pieces[g])
        rhs = jnp.concatenate([shi, shi, slo, slo], axis=0)
        basis[:, g * width : (g + 1) * width] = jnp.dot(lhs, rhs, preferred_element_type=F32)


def finish_kernel(core, lower, mine, other, out):
    size, cols = out.shape
    half = cols // LANES // 2
    is_first = core[0] == 0
    hi, lo = split2(lower[...])
    lhs = jnp.concatenate([hi, lo, hi, lo], axis=1)
    low, high = [], []
    for b in range(half):
        m, o = mine[b * size : (b + 1) * size], other[b * size : (b + 1) * size]
        low.append(jnp.where(is_first, m, o))
        high.append(jnp.where(is_first, o, m))
    shi, slo = split2(jnp.concatenate(low + high, axis=1))
    rhs = jnp.concatenate([shi, shi, slo, slo], axis=0)
    out[...] = jnp.dot(lhs, rhs, preferred_element_type=F32)


def call(kernel, name, out_shape, in_specs, limit=8, scratch=()):
    single = not isinstance(out_shape, tuple)
    return pl.pallas_call(
        kernel,
        out_shape=out_shape,
        in_specs=in_specs,
        out_specs=VM if single else (VM,) * len(out_shape),
        scratch_shapes=scratch,
        compiler_params=pltpu.CompilerParams(vmem_limit_bytes=limit * 2**20),
        name=name,
    )


def per_device(exposure, scales, sketch):
    rows, cols = exposure.shape
    size = sketch.shape[0]
    blocks = scales.shape[0]
    n_col = lax.axis_size(("y", "x"))
    n_z = lax.axis_size("z")
    width = rows // n_col
    half = blocks // 2 * size
    tall = half + size * size // LANES
    total_paths = rows * n_z * lax.axis_size("core")
    core = lax.axis_index("core").astype(jnp.int32).reshape(1)
    swap = [(0, 1), (1, 0)]
    shape = jax.ShapeDtypeStruct
    DMA = pltpu.SemaphoreType.DMA

    partial = call(
        sketch_kernel, "sketch", shape((n_col, size, width), F32), [ANY] * 3, 40,
        [
            pltpu.VMEM((size, cols), BF), pltpu.VMEM((blocks, rows), F32), pltpu.VMEM((rows, cols), BF),
            pltpu.VMEM((blocks * size, cols), BF), DMA((CHUNKS,)), DMA((2,)),
        ],
    )(sketch, scales, exposure)
    got = lax.all_to_all(partial, ("y", "x"), 0, 0)
    spread = call(sum_copies_kernel, "sum_parts", shape((n_col, size, width), F32), [VM])(got)
    pieces = lax.all_to_all(spread, ("y", "x"), 0, 0)

    mine, other = call(
        project_kernel, "project", (shape((tall, LANES), F32),) * 2, [SM, VM, ANY, ANY], 40,
        [
            pltpu.VMEM((blocks, rows), F32), pltpu.VMEM((rows, cols), BF), pltpu.VMEM((2 * size, rows), BF),
            pltpu.VMEM((2 * size * blocks, rows), BF), pltpu.VMEM((blocks, size, LANES), F32),
            DMA((CHUNKS,)), DMA((1,)),
        ],
    )(core, pieces, scales, exposure)

    received = lax.ppermute(other, "core", swap)
    spread_z = call(add_copies_kernel, "add_cores", shape((n_z, tall, LANES), F32), [VM, VM])(mine, received)
    got_z = lax.all_to_all(spread_z, "z", 0, 0)
    total = call(sum_kernel, "sum_z", shape((tall, LANES), F32), [VM])(got_z)
    total_other = lax.ppermute(total, "core", swap)
    lower, basis = call(
        functools.partial(solve_kernel, float(total_paths) ** 0.5), "solve",
        (shape((size, size), F32), shape((size, rows), F32)), [VM, VM],
    )(total, pieces)
    projected = call(finish_kernel, "finish", shape((size, cols), F32), [SM, VM, VM, VM])(
        core, lower, total, total_other
    )
    return (basis, projected)


def solution(mesh):
    path, col = ("z", "core"), ("y", "x")
    n_path, n_col = mesh.shape["path"], mesh.shape["col"]
    split = jax.sharding.Mesh(mesh.devices.reshape(n_path // 2, 2, 4, n_col // 4), path + col)
    return jax.shard_map(
        per_device,
        mesh=split,
        in_specs=(P(path, col), P(col, path), P(None, col)),
        out_specs=(P(None, path), P(None, col)),
        check_vma=False,
    )
```

time: 294 us -> 85.2 us (0.29)
  waiting for transfers between devices: 207 us -> 10.6 us
  matrix products: 17.8 us -> 0 us
  between operations: 14.1 us -> 0.68 us
  Pallas kernels: 0 us -> 13.4 us
  starting transfers between devices: 0.08 us -> 7.99 us
  other arithmetic: 6.69 us -> 0 us
  local copies, waits for them, and re-layouts: 3.09 us -> 8.51 us
    psum x2 -> x0, waiting for transfers between devices: 207 us -> none  [the longest x1 109 us: per_device(): projected = lax.psum(local_proj, 'path')]
    psum x1 -> x0, blocking collectives: 45.4 us -> none  [per_device(): gram_total = lax.psum(jnp.dot(sketched, sketched.T, precision=HIGH), 'path')]
    all_to_all x0 -> x2, blocking collectives: none -> 43.6 us  [the longest x1 25.7 us: per_device(): got_z = lax.all_to_all(spread_z, 'z', 0, 0)]
    dot_general x3 -> x0, matrix products: 15.3 us -> none  [the longest x1 7.25 us: per_device(): lax.dot_general(sketch3, codes, (((2,), (2,)), ((1,), (1,))), preferred_e...]
    pallas_call x0 -> x7, Pallas kernels: none -> 13.4 us  [the longest x1 4 us: per_device(): call(project_kernel, 'project', (shape((tall, LANES), F32),) * 2, [SM, VM...]
    all_to_all x0 -> x1, waiting for transfers between devices: none -> 9.66 us  [per_device(): pieces = lax.all_to_all(spread, ('y', 'x'), 0, 0)]
    another operation x5 -> x0, other arithmetic: 6.68 us -> none  [the longest x3 3.59 us: per_device(): factor = jnp.linalg.cholesky(gram_total)]
    unnamed x5 -> x10, local copies, waits for them, and re-layouts: 2.35 us -> 8.51 us
  transfers between devices with their start and end apart: 2 -> 3, of which waited for: 2 -> 2; matrix products, arithmetic and copies ran while one was open for 0% -> 0% of each run, Pallas kernels for 0% -> 4%
where the time goes in v2:
time: 85.2 us; the launch traced here: 84.8 us
  blocking collectives  43.6 us (51%)
  Pallas kernels  13.4 us (16%)
  waiting for transfers between devices  10.6 us (12%)
  local copies, waits for them, and re-layouts  8.51 us (10%)
  starting transfers between devices  7.99 us (9%)
    all_to_all x1, blocking collectives, per_device(): got_z = lax.all_to_all(spread_z, 'z', 0, 0)  25.7 us
    all_to_all x1, blocking collectives, per_device(): got = lax.all_to_all(partial, ('y', 'x'), 0, 0)  17.9 us
    all_to_all x1, waiting for transfers between devices, per_device(): pieces = lax.all_to_all(spread, ('y', 'x'), 0, 0)  9.66 us
    unnamed x10, local copies, waits for them, and re-layouts  8.51 us
    pallas_call x1, Pallas kernels, per_device(): call(project_kernel, 'project', (shape((tall, LANES), F32),) * 2, [SM, VM...  4 us
    pallas_call x1, Pallas kernels, per_device(): call(sketch_kernel, 'sketch', shape((n_col, size, width), F32), [ANY] * 3...  3.86 us
    pallas_call x1, Pallas kernels, per_device(): call(functools.partial(solve_kernel, float(total_paths) ** 0.5), 'solve',...  3.73 us
    all_to_all x1, starting transfers between devices, per_device(): pieces = lax.all_to_all(spread, ('y', 'x'), 0, 0)  3.57 us
  transfers between devices with their start and end apart: 3, of which 2 were waited for; matrix products, arithmetic and copies ran while one was open for 0% of the time, Pallas kernels for 4%

profile of v2, /device:TPU:1, one launch (start us, length us, event | category | flops | bytes accessed | tf_op | source)
XLA Modules:
  0.0 84.8 jit_solution(13857947493715356466)
XLA Ops:
  0.6 0.0 copy-start
  0.6 3.4 %copy-done = bf16[4096,1024]{1,0:T(8,128)(2,1)S(1)} copy-done((bf16[4096,1024]{1,0:T(8,128)(2,1)S(1)}, bf16[4096,1024]{1,0:T(8,128)(2,1)}, u32[]{:S(2)}) %copy-start) | copy-done | bytes 8388632
  4.0 0.0 copy-start.2
  4.0 0.9 %copy-done.2 = f32[8,4096]{1,0:T(8,128)S(1)} copy-done((f32[8,4096]{1,0:T(8,128)S(1)}, f32[8,4096]{1,0:T(8,128)}, u32[]{:S(2)}) %copy-start.2) | copy-done | bytes 131096
  4.9 0.0 copy-start.4
  4.9 0.8 copy-done.4
  5.8 0.0 copy-start.3
  5.8 3.9 %sketch.1 = f32[16,32,256]{2,1,0:T(8,128)S(1)} custom-call(bf16[32,1024]{1,0:T(8,128)(2,1)S(1)} %copy-done.4, f32[8,4096]{1,0:T(8,128)S(1)} %copy-done.2, bf16[4096,1024]{1,0:T(8,128)(2,1)S(1)} %copy-done), custom_call_target="tpu_custom_call" | custom-call | tf_op jit(solution)/shard_map/sketch/pallas_call | solution.py:201
  9.6 17.9 %all_to_all.15.x = f32[16,32,256]{2,1,0:T(8,128)S(1)} all-to-all(f32[16,32,256]{2,1,0:T(8,128)S(1)} %sketch.1), channel_id=1, replica_groups=mesh['z'=8,'core'=2,'y'=4,'x'=4] {'y','x'}, dimensions={0} | all-to-all | bytes 1048576 | tf_op jit(solution)/shard_map/all_to_all | solution.py:208
  27.5 0.9 %sum_parts.1 = f32[16,32,256]{2,1,0:T(8,128)} custom-call(f32[16,32,256]{2,1,0:T(8,128)S(1)} %all_to_all.15.x), custom_call_target="tpu_custom_call" | custom-call | tf_op jit(solution)/shard_map/sum_parts/pallas_call | solution.py:209
  28.4 3.6 %all-to-all-start.1 = ((f32[16,32,256]{2,1,0:T(8,128)}), f32[16,32,256]{2,1,0:T(8,128)S(1)}, u32[]{:S(2)}, u32[]{:S(2)}) async-start(f32[16,32,256]{2,1,0:T(8,128)} %sum_parts.1), calls=%async_computation.1 | async-start | bytes 1048576 | tf_op jit(solution)/shard_map/all_to_all | solution.py:210
  32.0 9.7 %all-to-all-done.1.pieces = f32[16,32,256]{2,1,0:T(8,128)S(1)} async-done(((f32[16,32,256]{2,1,0:T(8,128)}), f32[16,32,256]{2,1,0:T(8,128)S(1)}, u32[]{:S(2)}, u32[]{:S(2)}) %all-to-all-start.1) | async-done | bytes 524320 | tf_op jit(solution)/shard_map/all_to_all | solution.py:210
  41.6 0.0 copy-done.3
  41.6 0.0 copy-start.1
  41.6 3.4 %copy-done.1 = bf16[4096,1024]{1,0:T(8,128)(2,1)S(1)} copy-done((bf16[4096,1024]{1,0:T(8,128)(2,1)S(1)}, bf16[4096,1024]{1,0:T(8,128)(2,1)}, u32[]{:S(2)}) %copy-start.1) | copy-done | bytes 8388632
  45.0 4.0 %project.1 = (f32[136,128]{1,0:T(8,128)S(1)}, f32[136,128]{1,0:T(8,128)S(1)}) custom-call(s32[1]{0:T(128)} %bitcast.core, f32[16,32,256]{2,1,0:T(8,128)S(1)} %all-to-all-done.1.pieces, f32[8,4096]{1,0:T(8,128)S(1)} %copy-done.3, bf16[4096,1024]{1,0:T(8,128)(2,1)S(1)} %copy-done.1), custom_call_target="tpu_custom_call" | custom-call | tf_op jit(solution)/shard_map/project/pallas_call | solution.py:212
  49.0 2.9 %collective-permute-start = (f32[136,128]{1,0:T(8,128)S(1)}, f32[136,128]{1,0:T(8,128)S(1)}, u32[]{:S(2)}, u32[]{:S(2)}) collective-permute-start(f32[136,128]{1,0:T(8,128)S(1)} %get-tuple-element.7), channel_id=1, source_target_pairs={{0,16},{16,0},{1,17},{17,1},{2,18},{18,2},{3,19},{19,3},{4,20},{20... | collective-permute-start | bytes 208904 | tf_op jit(solution)/shard_map/ppermute | solution.py:221
  52.0 0.9 %collective-permute-done.b = f32[136,128]{1,0:T(8,128)S(1)} collective-permute-done((f32[136,128]{1,0:T(8,128)S(1)}, f32[136,128]{1,0:T(8,128)S(1)}, u32[]{:S(2)}, u32[]{:S(2)}) %collective-permute-start) | collective-permute-done | bytes 69664 | tf_op jit(solution)/shard_map/ppermute | solution.py:221
  52.9 25.7 %all_to_all.16.x = f32[8,136,128]{2,1,0:T(8,128)S(1)} all-to-all(f32[8,136,128]{2,1,0:T(8,128)S(1)} %add_cores.1), channel_id=1, replica_groups=mesh['z'=8,'core'=2,'y'=4,'x'=4] {'z'}, dimensions={0} | all-to-all | bytes 1114112 | tf_op jit(solution)/shard_map/all_to_all | solution.py:223
  78.7 1.5 %collective-permute-start.1 = (f32[136,128]{1,0:T(8,128)S(1)}, f32[136,128]{1,0:T(8,128)S(1)}, u32[]{:S(2)}, u32[]{:S(2)}) collective-permute-start(f32[136,128]{1,0:T(8,128)S(1)} %sum_z.1.x.mine), channel_id=1, source_target_pairs={{0,16},{16,0},{1,17},{17,1},{2,18},{18,2},{3,19},{19,3},{4,20},{20... | collective-permute-start | bytes 208904 | tf_op jit(solution)/shard_map/ppermute | solution.py:225
  80.2 3.7 %solve.1 = (f32[32,32]{1,0:T(8,128)S(1)}, f32[32,4096]{1,0:T(8,128)}) custom-call(f32[136,128]{1,0:T(8,128)S(1)} %sum_z.1.x.mine, f32[16,32,256]{2,1,0:T(8,128)S(1)} %all-to-all-done.1.pieces), custom_call_target="tpu_custom_call" | custom-call | tf_op jit(solution)/shard_map/solve/pallas_call | solution.py:226
  83.9 0.0 collective-permute-done.1.other
  83.9 0.9 %finish.1 = f32[32,1024]{1,0:T(8,128)} custom-call(s32[1]{0:T(128)} %bitcast.core, f32[32,32]{1,0:T(8,128)S(1)} %get-tuple-element.9.lower, f32[136,128]{1,0:T(8,128)S(1)} %sum_z.1.x.mine, f32[136,128]{1,0:T(8,128)S(1)} %collective-permute-done.1.other), custom_call_target="tpu_custom_call" | custom-call | tf_op jit(solution)/shard_map/finish/pallas_call | solution.py:230
  (2 shorter events, 0.1 us)
Async XLA Ops:
  0.6 3.4 %copy-start = (bf16[4096,1024]{1,0:T(8,128)(2,1)S(1)}, bf16[4096,1024]{1,0:T(8,128)(2,1)}, u32[]{:S(2)}) copy-start(bf16[4096,1024]{1,0:T(8,128)(2,1)} %exposure.3) | copy-start | bytes 25165828
  4.0 0.9 %copy-start.2 = (f32[8,4096]{1,0:T(8,128)S(1)}, f32[8,4096]{1,0:T(8,128)}, u32[]{:S(2)}) copy-start(f32[8,4096]{1,0:T(8,128)} %scales_hbm.3) | copy-start | bytes 393220
  4.9 0.8 copy-start.4
  5.8 35.9 %copy-start.3 = (f32[8,4096]{1,0:T(8,128)S(1)}, f32[8,4096]{1,0:T(8,128)}, u32[]{:S(2)}) copy-start(f32[8,4096]{1,0:T(8,128)} %scales_hbm.3) | copy-start | bytes 393220
  28.4 13.2 %all-to-all-start.1 = ((f32[16,32,256]{2,1,0:T(8,128)}), f32[16,32,256]{2,1,0:T(8,128)S(1)}, u32[]{:S(2)}, u32[]{:S(2)}) async-start(f32[16,32,256]{2,1,0:T(8,128)} %sum_parts.1), calls=%async_computation.1 | async-start | bytes 1048576 | tf_op jit(solution)/shard_map/all_to_all | solution.py:210
  41.6 3.4 %copy-start.1 = (bf16[4096,1024]{1,0:T(8,128)(2,1)S(1)}, bf16[4096,1024]{1,0:T(8,128)(2,1)}, u32[]{:S(2)}) copy-start(bf16[4096,1024]{1,0:T(8,128)(2,1)} %exposure.3) | copy-start | bytes 25165828
  49.0 3.8 %collective-permute-start = (f32[136,128]{1,0:T(8,128)S(1)}, f32[136,128]{1,0:T(8,128)S(1)}, u32[]{:S(2)}, u32[]{:S(2)}) collective-permute-start(f32[136,128]{1,0:T(8,128)S(1)} %get-tuple-element.7), channel_id=1, source_target_pairs={{0,16},{16,0},{1,17},{17,1},{2,18},{18,2},{3,19},{19,3},{4,20},{20... | collective-permute-start | bytes 208904 | tf_op jit(solution)/shard_map/ppermute | solution.py:221
  78.7 5.2 %collective-permute-start.1 = (f32[136,128]{1,0:T(8,128)S(1)}, f32[136,128]{1,0:T(8,128)S(1)}, u32[]{:S(2)}, u32[]{:S(2)}) collective-permute-start(f32[136,128]{1,0:T(8,128)S(1)} %sum_z.1.x.mine), channel_id=1, source_target_pairs={{0,16},{16,0},{1,17},{17,1},{2,18},{18,2},{3,19},{19,3},{4,20},{20... | collective-permute-start | bytes 208904 | tf_op jit(solution)/shard_map/ppermute | solution.py:225

commit v3 on v2

--- a/solution.py
+++ b/solution.py
@@ -8,10 +8,11 @@
 
 BF = jnp.bfloat16
 F32 = jnp.float32
-ANY = pl.BlockSpec(memory_space=pl.ANY)
+HBM = pl.BlockSpec(memory_space=pltpu.HBM)
 VM = pl.BlockSpec(memory_space=pltpu.VMEM)
-SM = pl.BlockSpec(memory_space=pltpu.SMEM)
 CHUNKS = 4
+AHEAD = 2
+PANEL = 8
 LANES = 128
 NT = (((1,), (1,)), ((), ()))
 
@@ -25,17 +26,7 @@
     return slice(b * LANES, (b + n) * LANES)
 
 
-def fetch(exposure, held, sems):
-    step = held.shape[0] // CHUNKS
-    copies = []
-    for c in range(CHUNKS):
-        part = pl.ds(c * step, step)
-        copies.append(pltpu.make_async_copy(exposure.at[part], held.at[part], sems.at[c]))
-        copies[-1].start()
-    return copies
-
-
-def sketch_kernel(sketch_hbm, scales_hbm, exposure, out, sketch, scales, held, diag, sems, small):
+def sketch_kernel(sketch_hbm, scales_hbm, exposure, out, held, sketch, scales, diag, sems, small):
     size = sketch.shape[0]
     blocks = scales.shape[0]
     groups, _, width = out.shape
@@ -44,7 +35,13 @@
     second = pltpu.make_async_copy(scales_hbm, scales, small.at[1])
     first.start()
     second.start()
-    copies = fetch(exposure, held, sems)
+    step = held.shape[0] // CHUNKS
+    copies = []
+    for c in range(CHUNKS):
+        part = pl.ds(c * step, step)
+        copies.append(pltpu.make_async_copy(exposure.at[part], held.at[part], sems.at[c]))
+    for copy in copies[:AHEAD]:
+        copy.start()
     diag[...] = jnp.zeros_like(diag)
     first.wait()
     for b in range(blocks):
@@ -52,6 +49,8 @@
     second.wait()
     for c in range(CHUNKS):
         copies[c].wait()
+        if c + AHEAD < CHUNKS:
+            copies[c + AHEAD].start()
         for g in range(c * per_chunk, (c + 1) * per_chunk):
             span = slice(g * width, (g + 1) * width)
             parts = lax.dot_general(diag[...], held[span, :], NT, preferred_element_type=F32)
@@ -78,19 +77,15 @@
     out[...] = jnp.sum(x[...], axis=0)
 
 
-def project_kernel(core, pieces, scales_hbm, exposure, mine, other, scales, held, both, w, acc, sems, small):
+def project_kernel(pieces, scales, exposure, mine, other, both, w, acc):
     groups, size, width = pieces.shape
     blocks = scales.shape[0]
     per_chunk = groups // CHUNKS
-    step = held.shape[0] // CHUNKS
-    first = pltpu.make_async_copy(scales_hbm, scales, small.at[0])
-    first.start()
-    copies = fetch(exposure, held, sems)
+    step = exposure.shape[0] // CHUNKS
     for g in range(groups):
         both[:, g * width : (g + 1) * width] = jnp.concatenate(split2(pieces[g]), axis=0)
     gram = lax.dot_general(both[...], both[...], NT, preferred_element_type=F32)
     gram = (gram[:size, :size] + gram[size:, size:]) + (gram[:size, size:] + gram[size:, :size])
-    first.wait()
     for c in range(CHUNKS):
         for g in range(c * per_chunk, (c + 1) * per_chunk):
             span = slice(g * width, (g + 1) * width)
@@ -99,11 +94,10 @@
                 w[2 * size * b : 2 * size * (b + 1), span] = jnp.concatenate(
                     split2(s * scales[b : b + 1, span]), axis=0
                 )
-        copies[c].wait()
         rows = slice(c * step, (c + 1) * step)
         for b in range(0, blocks, 2):
             t = jnp.dot(
-                w[2 * size * b : 2 * size * (b + 2), rows], held[rows, lanes(b, 2)],
+                w[2 * size * b : 2 * size * (b + 2), rows], exposure[rows, lanes(b, 2)],
                 preferred_element_type=F32,
             )
             t0 = t[:size, :LANES] + t[size : 2 * size, :LANES]
@@ -116,7 +110,7 @@
                 acc[b + 1] += t1
 
     half = blocks // 2
-    is_first = core[0] == 0
+    is_first = lax.axis_index("core") == 0
     for b in range(half):
         low, high = acc[b], acc[half + b]
         mine[b * size : (b + 1) * size] = jnp.where(is_first, low, high)
@@ -137,13 +131,17 @@
     eye = jnp.where(lane - size == row, 1.0, 0.0).astype(F32)
     a = jnp.where(lane < size, jnp.pad(gram, ((0, 0), (0, LANES - size))), eye)
     inv = jnp.zeros((size, LANES), F32)
-    for j in range(size):
-        pivot_row = a[j : j + 1, :]
-        pivot = pivot_row[:, j : j + 1]
-        inv = jnp.where(row == j, pivot_row * lax.rsqrt(pivot), inv)
-        if j < size - 1:
-            col = a[:, j : j + 1]
-            a = a - jnp.where(row > j, (col / pivot) * pivot_row, 0.0)
+    for start in range(0, size, PANEL):
+        cols = [jnp.broadcast_to(a[:, j : j + 1], (size, LANES)) for j in range(start, start + PANEL)]
+        for k in range(PANEL):
+            j = start + k
+            pivot = cols[k][j : j + 1, :]
+            pivot_row = a[j : j + 1, :]
+            inv = jnp.where(row == j, pivot_row * lax.rsqrt(pivot), inv)
+            scaled = jnp.where(row > j, cols[k] * (1.0 / pivot), 0.0)
+            a = a - scaled * pivot_row
+            for m in range(k + 1, PANEL):
+                cols[m] = cols[m] - scaled * cols[m][j : j + 1, :]
     linv = inv[:, size : 2 * size]
     lower[...] = linv
     hi, lo = split2(linv * factor)
@@ -154,10 +152,10 @@
         basis[:, g * width : (g + 1) * width] = jnp.dot(lhs, rhs, preferred_element_type=F32)
 
 
-def finish_kernel(core, lower, mine, other, out):
+def finish_kernel(lower, mine, other, out):
     size, cols = out.shape
     half = cols // LANES // 2
-    is_first = core[0] == 0
+    is_first = lax.axis_index("core") == 0
     hi, lo = split2(lower[...])
     lhs = jnp.concatenate([hi, lo, hi, lo], axis=1)
     low, high = [], []
@@ -193,30 +191,29 @@
     half = blocks // 2 * size
     tall = half + size * size // LANES
     total_paths = rows * n_z * lax.axis_size("core")
-    core = lax.axis_index("core").astype(jnp.int32).reshape(1)
     swap = [(0, 1), (1, 0)]
     shape = jax.ShapeDtypeStruct
     DMA = pltpu.SemaphoreType.DMA
 
-    partial = call(
-        sketch_kernel, "sketch", shape((n_col, size, width), F32), [ANY] * 3, 40,
+    partial, held = call(
+        sketch_kernel, "sketch", (shape((n_col, size, width), F32), pltpu.VMEM((rows, cols), BF)),
+        [HBM] * 3, 40,
         [
-            pltpu.VMEM((size, cols), BF), pltpu.VMEM((blocks, rows), F32), pltpu.VMEM((rows, cols), BF),
+            pltpu.VMEM((size, cols), BF), pltpu.VMEM((blocks, rows), F32),
             pltpu.VMEM((blocks * size, cols), BF), DMA((CHUNKS,)), DMA((2,)),
         ],
-    )(sketch, scales, exposure)
+    )(*(pltpu.with_memory_space_constraint(x, pltpu.HBM) for x in (sketch, scales, exposure)))
     got = lax.all_to_all(partial, ("y", "x"), 0, 0)
     spread = call(sum_copies_kernel, "sum_parts", shape((n_col, size, width), F32), [VM])(got)
     pieces = lax.all_to_all(spread, ("y", "x"), 0, 0)
 
     mine, other = call(
-        project_kernel, "project", (shape((tall, LANES), F32),) * 2, [SM, VM, ANY, ANY], 40,
+        project_kernel, "project", (shape((tall, LANES), F32),) * 2, [VM, VM, VM], 40,
         [
-            pltpu.VMEM((blocks, rows), F32), pltpu.VMEM((rows, cols), BF), pltpu.VMEM((2 * size, rows), BF),
-            pltpu.VMEM((2 * size * blocks, rows), BF), pltpu.VMEM((blocks, size, LANES), F32),
-            DMA((CHUNKS,)), DMA((1,)),
+            pltpu.VMEM((2 * size, rows), BF), pltpu.VMEM((2 * size * blocks, rows), BF),
+            pltpu.VMEM((blocks, size, LANES), F32),
         ],
-    )(core, pieces, scales, exposure)
+    )(pieces, scales, held)
 
     received = lax.ppermute(other, "core", swap)
     spread_z = call(add_copies_kernel, "add_cores", shape((n_z, tall, LANES), F32), [VM, VM])(mine, received)
@@ -227,8 +224,8 @@
         functools.partial(solve_kernel, float(total_paths) ** 0.5), "solve",
         (shape((size, size), F32), shape((size, rows), F32)), [VM, VM],
     )(total, pieces)
-    projected = call(finish_kernel, "finish", shape((size, cols), F32), [SM, VM, VM, VM])(
-        core, lower, total, total_other
+    projected = call(finish_kernel, "finish", shape((size, cols), F32), [VM, VM, VM])(
+        lower, total, total_other
     )
     return (basis, projected)
 

time: 85.2 us -> 72.3 us (0.85)
  blocking collectives: 43.6 us -> 56.7 us
  waiting for transfers between devices: 10.6 us -> 0.91 us
  local copies, waits for them, and re-layouts: 8.51 us -> 0.01 us
  starting transfers between devices: 7.99 us -> 4.15 us
  Pallas kernels: 13.4 us -> 9.64 us
    all_to_all x0 -> x1, blocking collectives: none -> 13.1 us  [per_device(): pieces = lax.all_to_all(spread, ('y', 'x'), 0, 0)]
    all_to_all x1 -> x0, waiting for transfers between devices: 9.66 us -> none  [per_device(): pieces = lax.all_to_all(spread, ('y', 'x'), 0, 0)]
    unnamed x10 -> x2, local copies, waits for them, and re-layouts: 8.51 us -> 0.01 us
    all_to_all x1 -> x0, starting transfers between devices: 3.57 us -> none  [per_device(): pieces = lax.all_to_all(spread, ('y', 'x'), 0, 0)]
    pallas_call x1, Pallas kernels: 3.73 us -> 1.89 us  [per_device(): call(functools.partial(solve_kernel, float(total_paths) ** 0.5), 'solve',...]
    pallas_call x3, Pallas kernels: 8.74 us -> 7.62 us  [the longest x1 5.27 us: per_device(): call(sketch_kernel, 'sketch', (shape((n_col, size, width), F32), pltpu.VM...]
  transfers between devices with their start and end apart: 3 -> 2, of which waited for: 2 -> 1; matrix products, arithmetic and copies ran while one was open for 0% -> 0% of each run, Pallas kernels for 4% -> 3%
where the time goes in v3:
time: 72.3 us; the launch traced here: 72.1 us
  blocking collectives  56.7 us (78%)
  Pallas kernels  9.64 us (13%)
  starting transfers between devices  4.15 us (6%)
  waiting for transfers between devices  0.91 us (1%)
    all_to_all x1, blocking collectives, per_device(): got_z = lax.all_to_all(spread_z, 'z', 0, 0)  25.7 us
    all_to_all x1, blocking collectives, per_device(): got = lax.all_to_all(partial, ('y', 'x'), 0, 0)  17.9 us
    all_to_all x1, blocking collectives, per_device(): pieces = lax.all_to_all(spread, ('y', 'x'), 0, 0)  13.1 us
    pallas_call x1, Pallas kernels, per_device(): call(sketch_kernel, 'sketch', (shape((n_col, size, width), F32), pltpu.VM...  5.27 us
    ppermute x1, starting transfers between devices, per_device(): received = lax.ppermute(other, 'core', swap)  2.66 us
    pallas_call x1, Pallas kernels, per_device(): call(functools.partial(solve_kernel, float(total_paths) ** 0.5), 'solve',...  1.89 us
    ppermute x1, starting transfers between devices, per_device(): total_other = lax.ppermute(total, 'core', swap)  1.49 us
    pallas_call x1, Pallas kernels, per_device(): call(project_kernel, 'project', (shape((tall, LANES), F32),) * 2, [VM, VM...  1.48 us
  transfers between devices with their start and end apart: 2, of which 1 were waited for; matrix products, arithmetic and copies ran while one was open for 0% of the time, Pallas kernels for 3%

profile of v3, /device:TPU:1, one launch (start us, length us, event | category | flops | bytes accessed | tf_op | source)
XLA Modules:
  0.0 72.1 jit_solution(16322821288185899907)
XLA Ops:
  0.6 0.0 copy-start
  0.6 5.3 %sketch.1 = (f32[16,32,256]{2,1,0:T(8,128)S(1)}, bf16[4096,1024]{1,0:T(8,128)(2,1)S(1)}) custom-call(bf16[32,1024]{1,0:T(8,128)(2,1)} %sketch_hbm.1, f32[8,4096]{1,0:T(8,128)} %scales.1, bf16[4096,1024]{1,0:T(8,128)(2,1)} %exposure.1), custom_call_target="tpu_custom_call" | custom-call | tf_op jit(solution)/shard_map/sketch/pallas_call | solution.py:198
  5.9 17.9 %all_to_all.15.x = f32[16,32,256]{2,1,0:T(8,128)S(1)} all-to-all(f32[16,32,256]{2,1,0:T(8,128)S(1)} %get-tuple-element.8), channel_id=1, replica_groups=mesh['z'=8,'core'=2,'y'=4,'x'=4] {'y','x'}, dimensions={0} | all-to-all | bytes 1048576 | tf_op jit(solution)/shard_map/all_to_all | solution.py:206
  23.8 0.1 sum_parts.1
  23.9 13.1 %all_to_all.16.pieces = f32[16,32,256]{2,1,0:T(8,128)S(1)} all-to-all(f32[16,32,256]{2,1,0:T(8,128)S(1)} %sum_parts.1), channel_id=1, replica_groups=mesh['z'=8,'core'=2,'y'=4,'x'=4] {'y','x'}, dimensions={0} | all-to-all | bytes 1048576 | tf_op jit(solution)/shard_map/all_to_all | solution.py:208
  37.0 0.0 copy-done
  37.0 1.5 %project.1 = (f32[136,128]{1,0:T(8,128)S(1)}, f32[136,128]{1,0:T(8,128)S(1)}) custom-call(f32[16,32,256]{2,1,0:T(8,128)S(1)} %all_to_all.16.pieces, f32[8,4096]{1,0:T(8,128)S(1)} %copy-done, bf16[4096,1024]{1,0:T(8,128)(2,1)S(1)} %get-tuple-element.9.exposure), custom_call_target="tpu_custom_call" | custom-call | tf_op jit(solution)/shard_map/project/pallas_call | solution.py:210
  38.5 2.7 %collective-permute-start = (f32[136,128]{1,0:T(8,128)S(1)}, f32[136,128]{1,0:T(8,128)S(1)}, u32[]{:S(2)}, u32[]{:S(2)}) collective-permute-start(f32[136,128]{1,0:T(8,128)S(1)} %get-tuple-element.11), channel_id=1, source_target_pairs={{0,16},{16,0},{1,17},{17,1},{2,18},{18,2},{3,19},{19,3},{4,20},{20... | collective-permute-start | bytes 208904 | tf_op jit(solution)/shard_map/ppermute | solution.py:218
  41.1 0.9 %collective-permute-done.b = f32[136,128]{1,0:T(8,128)S(1)} collective-permute-done((f32[136,128]{1,0:T(8,128)S(1)}, f32[136,128]{1,0:T(8,128)S(1)}, u32[]{:S(2)}, u32[]{:S(2)}) %collective-permute-start) | collective-permute-done | bytes 69664 | tf_op jit(solution)/shard_map/ppermute | solution.py:218
  42.1 25.7 %all_to_all.17.x = f32[8,136,128]{2,1,0:T(8,128)S(1)} all-to-all(f32[8,136,128]{2,1,0:T(8,128)S(1)} %add_cores.1), channel_id=1, replica_groups=mesh['z'=8,'core'=2,'y'=4,'x'=4] {'z'}, dimensions={0} | all-to-all | bytes 1114112 | tf_op jit(solution)/shard_map/all_to_all | solution.py:220
  67.8 1.5 %collective-permute-start.1 = (f32[136,128]{1,0:T(8,128)S(1)}, f32[136,128]{1,0:T(8,128)S(1)}, u32[]{:S(2)}, u32[]{:S(2)}) collective-permute-start(f32[136,128]{1,0:T(8,128)S(1)} %sum_z.1.x.mine), channel_id=1, source_target_pairs={{0,16},{16,0},{1,17},{17,1},{2,18},{18,2},{3,19},{19,3},{4,20},{20... | collective-permute-start | bytes 208904 | tf_op jit(solution)/shard_map/ppermute | solution.py:222
  69.3 1.9 %solve.1 = (f32[32,32]{1,0:T(8,128)S(1)}, f32[32,4096]{1,0:T(8,128)}) custom-call(f32[136,128]{1,0:T(8,128)S(1)} %sum_z.1.x.mine, f32[16,32,256]{2,1,0:T(8,128)S(1)} %all_to_all.16.pieces), custom_call_target="tpu_custom_call" | custom-call | tf_op jit(solution)/shard_map/solve/pallas_call | solution.py:223
  71.2 0.0 collective-permute-done.1.other
  71.2 0.9 %finish.1 = f32[32,1024]{1,0:T(8,128)} custom-call(f32[32,32]{1,0:T(8,128)S(1)} %get-tuple-element.13.lower, f32[136,128]{1,0:T(8,128)S(1)} %sum_z.1.x.mine, f32[136,128]{1,0:T(8,128)S(1)} %collective-permute-done.1.other), custom_call_target="tpu_custom_call" | custom-call | tf_op jit(solution)/shard_map/finish/pallas_call | solution.py:227
  (2 shorter events, 0.1 us)
Async XLA Ops:
  0.6 36.3 %copy-start = (f32[8,4096]{1,0:T(8,128)S(1)}, f32[8,4096]{1,0:T(8,128)}, u32[]{:S(2)}) copy-start(f32[8,4096]{1,0:T(8,128)} %scales.1) | copy-start | bytes 393220
  38.5 3.6 %collective-permute-start = (f32[136,128]{1,0:T(8,128)S(1)}, f32[136,128]{1,0:T(8,128)S(1)}, u32[]{:S(2)}, u32[]{:S(2)}) collective-permute-start(f32[136,128]{1,0:T(8,128)S(1)} %get-tuple-element.11), channel_id=1, source_target_pairs={{0,16},{16,0},{1,17},{17,1},{2,18},{18,2},{3,19},{19,3},{4,20},{20... | collective-permute-start | bytes 208904 | tf_op jit(solution)/shard_map/ppermute | solution.py:218
  67.8 3.4 %collective-permute-start.1 = (f32[136,128]{1,0:T(8,128)S(1)}, f32[136,128]{1,0:T(8,128)S(1)}, u32[]{:S(2)}, u32[]{:S(2)}) collective-permute-start(f32[136,128]{1,0:T(8,128)S(1)} %sum_z.1.x.mine), channel_id=1, source_target_pairs={{0,16},{16,0},{1,17},{17,1},{2,18},{18,2},{3,19},{19,3},{4,20},{20... | collective-permute-start | bytes 208904 | tf_op jit(solution)/shard_map/ppermute | solution.py:222

commit v4 on v3

--- a/solution.py
+++ b/solution.py
@@ -11,6 +11,12 @@
 HBM = pl.BlockSpec(memory_space=pltpu.HBM)
 VM = pl.BlockSpec(memory_space=pltpu.VMEM)
 CHUNKS = 4
+PAIRS = {
+    "a": ((0, 1), (2, 3), (4, 5), (6, 7)),
+    "b": ((1, 2), (3, 4), (5, 6), (7, 0)),
+    "c": ((0, 3), (1, 6), (2, 5), (4, 7)),
+}
+ORDER = "cba"
 AHEAD = 2
 PANEL = 8
 LANES = 128
@@ -67,14 +73,8 @@
         out[j] = total
 
 
-def add_copies_kernel(a, b, out):
-    total = a[...] + b[...]
-    for j in range(out.shape[0]):
-        out[j] = total
-
-
-def sum_kernel(x, out):
-    out[...] = jnp.sum(x[...], axis=0)
+def add_kernel(a, b, out):
+    out[...] = a[...] + b[...]
 
 
 def project_kernel(pieces, scales, exposure, mine, other, both, w, acc):
@@ -215,10 +215,11 @@
         ],
     )(pieces, scales, held)
 
-    received = lax.ppermute(other, "core", swap)
-    spread_z = call(add_copies_kernel, "add_cores", shape((n_z, tall, LANES), F32), [VM, VM])(mine, received)
-    got_z = lax.all_to_all(spread_z, "z", 0, 0)
-    total = call(sum_kernel, "sum_z", shape((tall, LANES), F32), [VM])(got_z)
+    add = call(add_kernel, "add", shape((tall, LANES), F32), [VM, VM])
+    total = add(mine, lax.ppermute(other, "core", swap))
+    for step in ORDER:
+        both_ways = [p for i, j in PAIRS[step] for p in ((i, j), (j, i))]
+        total = add(total, lax.ppermute(total, "z", both_ways))
     total_other = lax.ppermute(total, "core", swap)
     lower, basis = call(
         functools.partial(solve_kernel, float(total_paths) ** 0.5), "solve",

time: 72.3 us -> 64.3 us (0.89)
  blocking collectives: 56.7 us -> 31 us
  starting transfers between devices: 4.15 us -> 15.2 us
  waiting for transfers between devices: 0.91 us -> 7.63 us
    all_to_all x1 -> x0, blocking collectives: 25.7 us -> none  [per_device(): got_z = lax.all_to_all(spread_z, 'z', 0, 0)]
    ppermute x1 -> x4, starting transfers between devices: 2.66 us -> 11.6 us  [the longest x3 8.93 us: per_device(): total = add(total, lax.ppermute(total, 'z', both_ways))]
    ppermute x1 -> x4, waiting for transfers between devices: 0.91 us -> 7.63 us  [the longest x3 6.72 us: per_device(): total = add(total, lax.ppermute(total, 'z', both_ways))]
    ppermute x1, starting transfers between devices: 1.49 us -> 3.61 us  [per_device(): total_other = lax.ppermute(total, 'core', swap)]
  transfers between devices with their start and end apart: 2 -> 5, of which waited for: 1 -> 4; matrix products, arithmetic and copies ran while one was open for 0% -> 0% of each run, Pallas kernels for 3% -> 3%
where the time goes in v4:
time: 64.3 us; the launch traced here: 64.1 us
  blocking collectives  31 us (48%)
  starting transfers between devices  15.2 us (24%)
  Pallas kernels  9.61 us (15%)
  waiting for transfers between devices  7.63 us (12%)
  between operations  0.68 us (1%)
    all_to_all x1, blocking collectives, per_device(): got = lax.all_to_all(partial, ('y', 'x'), 0, 0)  17.9 us
    all_to_all x1, blocking collectives, per_device(): pieces = lax.all_to_all(spread, ('y', 'x'), 0, 0)  13.1 us
    ppermute x3, starting transfers between devices, per_device(): total = add(total, lax.ppermute(total, 'z', both_ways))  8.93 us
    ppermute x3, waiting for transfers between devices, per_device(): total = add(total, lax.ppermute(total, 'z', both_ways))  6.72 us
    pallas_call x1, Pallas kernels, per_device(): call(sketch_kernel, 'sketch', (shape((n_col, size, width), F32), pltpu.VM...  5.27 us
    ppermute x1, starting transfers between devices, per_device(): total_other = lax.ppermute(total, 'core', swap)  3.61 us
    ppermute x1, starting transfers between devices, per_device(): total = add(mine, lax.ppermute(other, 'core', swap))  2.66 us
    pallas_call x1, Pallas kernels, per_device(): call(functools.partial(solve_kernel, float(total_paths) ** 0.5), 'solve',...  1.89 us
  transfers between devices with their start and end apart: 5, of which 4 were waited for; matrix products, arithmetic and copies ran while one was open for 0% of the time, Pallas kernels for 3%

profile of v4, /device:TPU:1, one launch (start us, length us, event | category | flops | bytes accessed | tf_op | source)
XLA Modules:
  0.0 64.1 jit_solution(11524658479720794860)
XLA Ops:
  0.6 0.0 copy-start
  0.6 5.3 %sketch.1 = (f32[16,32,256]{2,1,0:T(8,128)S(1)}, bf16[4096,1024]{1,0:T(8,128)(2,1)S(1)}) custom-call(bf16[32,1024]{1,0:T(8,128)(2,1)} %sketch_hbm.1, f32[8,4096]{1,0:T(8,128)} %scales.1, bf16[4096,1024]{1,0:T(8,128)(2,1)} %exposure.1), custom_call_target="tpu_custom_call" | custom-call | tf_op jit(solution)/shard_map/sketch/pallas_call | solution.py:198
  5.9 17.9 %all_to_all.10.x = f32[16,32,256]{2,1,0:T(8,128)S(1)} all-to-all(f32[16,32,256]{2,1,0:T(8,128)S(1)} %get-tuple-element.8), channel_id=1, replica_groups=mesh['z'=8,'core'=2,'y'=4,'x'=4] {'y','x'}, dimensions={0} | all-to-all | bytes 1048576 | tf_op jit(solution)/shard_map/all_to_all | solution.py:206
  23.8 0.1 sum_parts.1
  23.9 13.1 %all_to_all.11.pieces = f32[16,32,256]{2,1,0:T(8,128)S(1)} all-to-all(f32[16,32,256]{2,1,0:T(8,128)S(1)} %sum_parts.1), channel_id=1, replica_groups=mesh['z'=8,'core'=2,'y'=4,'x'=4] {'y','x'}, dimensions={0} | all-to-all | bytes 1048576 | tf_op jit(solution)/shard_map/all_to_all | solution.py:208
  37.0 0.0 copy-done
  37.0 1.5 %project.1 = (f32[136,128]{1,0:T(8,128)S(1)}, f32[136,128]{1,0:T(8,128)S(1)}) custom-call(f32[16,32,256]{2,1,0:T(8,128)S(1)} %all_to_all.11.pieces, f32[8,4096]{1,0:T(8,128)S(1)} %copy-done, bf16[4096,1024]{1,0:T(8,128)(2,1)S(1)} %get-tuple-element.9.exposure), custom_call_target="tpu_custom_call" | custom-call | tf_op jit(solution)/shard_map/project/pallas_call | solution.py:210
  38.5 2.7 %collective-permute-start = (f32[136,128]{1,0:T(8,128)S(1)}, f32[136,128]{1,0:T(8,128)S(1)}, u32[]{:S(2)}, u32[]{:S(2)}) collective-permute-start(f32[136,128]{1,0:T(8,128)S(1)} %get-tuple-element.11), channel_id=1, source_target_pairs={{0,16},{16,0},{1,17},{17,1},{2,18},{18,2},{3,19},{19,3},{4,20},{20... | collective-permute-start | bytes 208904 | tf_op jit(solution)/shard_map/ppermute | solution.py:219
  41.1 0.9 %collective-permute-done.b = f32[136,128]{1,0:T(8,128)S(1)} collective-permute-done((f32[136,128]{1,0:T(8,128)S(1)}, f32[136,128]{1,0:T(8,128)S(1)}, u32[]{:S(2)}, u32[]{:S(2)}) %collective-permute-start) | collective-permute-done | bytes 69664 | tf_op jit(solution)/shard_map/ppermute | solution.py:219
  42.0 4.4 %collective-permute-start.1 = (f32[136,128]{1,0:T(8,128)S(1)}, f32[136,128]{1,0:T(8,128)S(1)}, u32[]{:S(2)}, u32[]{:S(2)}) collective-permute-start(f32[136,128]{1,0:T(8,128)S(1)} %add.4.a), channel_id=1, source_target_pairs={{0,96},{96,0},{32,192},{192,32},{64,160},{160,64},{128,224},{224,1... | collective-permute-start | bytes 208904 | tf_op jit(solution)/shard_map/ppermute | solution.py:222
  46.5 2.3 %collective-permute-done.1.b = f32[136,128]{1,0:T(8,128)S(1)} collective-permute-done((f32[136,128]{1,0:T(8,128)S(1)}, f32[136,128]{1,0:T(8,128)S(1)}, u32[]{:S(2)}, u32[]{:S(2)}) %collective-permute-start.1) | collective-permute-done | bytes 69664 | tf_op jit(solution)/shard_map/ppermute | solution.py:222
  48.7 4.0 %collective-permute-start.2 = (f32[136,128]{1,0:T(8,128)S(1)}, f32[136,128]{1,0:T(8,128)S(1)}, u32[]{:S(2)}, u32[]{:S(2)}) collective-permute-start(f32[136,128]{1,0:T(8,128)S(1)} %add.5.a), channel_id=1, source_target_pairs={{32,64},{64,32},{96,128},{128,96},{160,192},{192,160},{224,0},{0,2... | collective-permute-start | bytes 208904 | tf_op jit(solution)/shard_map/ppermute | solution.py:222
  52.8 1.7 %collective-permute-done.2.b = f32[136,128]{1,0:T(8,128)S(1)} collective-permute-done((f32[136,128]{1,0:T(8,128)S(1)}, f32[136,128]{1,0:T(8,128)S(1)}, u32[]{:S(2)}, u32[]{:S(2)}) %collective-permute-start.2) | collective-permute-done | bytes 69664 | tf_op jit(solution)/shard_map/ppermute | solution.py:222
  54.5 0.5 collective-permute-start.3
  55.0 2.8 %collective-permute-done.3.b = f32[136,128]{1,0:T(8,128)S(1)} collective-permute-done((f32[136,128]{1,0:T(8,128)S(1)}, f32[136,128]{1,0:T(8,128)S(1)}, u32[]{:S(2)}, u32[]{:S(2)}) %collective-permute-start.3) | collective-permute-done | bytes 69664 | tf_op jit(solution)/shard_map/ppermute | solution.py:222
  57.7 3.6 %collective-permute-start.4 = (f32[136,128]{1,0:T(8,128)S(1)}, f32[136,128]{1,0:T(8,128)S(1)}, u32[]{:S(2)}, u32[]{:S(2)}) collective-permute-start(f32[136,128]{1,0:T(8,128)S(1)} %add.7.x.mine), channel_id=1, source_target_pairs={{0,16},{16,0},{1,17},{17,1},{2,18},{18,2},{3,19},{19,3},{4,20},{20... | collective-permute-start | bytes 208904 | tf_op jit(solution)/shard_map/ppermute | solution.py:223
  61.3 1.9 %solve.1 = (f32[32,32]{1,0:T(8,128)S(1)}, f32[32,4096]{1,0:T(8,128)}) custom-call(f32[136,128]{1,0:T(8,128)S(1)} %add.7.x.mine, f32[16,32,256]{2,1,0:T(8,128)S(1)} %all_to_all.11.pieces), custom_call_target="tpu_custom_call" | custom-call | tf_op jit(solution)/shard_map/solve/pallas_call | solution.py:224
  63.2 0.0 collective-permute-done.4.other
  63.2 0.9 %finish.1 = f32[32,1024]{1,0:T(8,128)} custom-call(f32[32,32]{1,0:T(8,128)S(1)} %get-tuple-element.13.lower, f32[136,128]{1,0:T(8,128)S(1)} %add.7.x.mine, f32[136,128]{1,0:T(8,128)S(1)} %collective-permute-done.4.other), custom_call_target="tpu_custom_call" | custom-call | tf_op jit(solution)/shard_map/finish/pallas_call | solution.py:228
  (4 shorter events, 0.0 us)
Async XLA Ops:
  0.6 36.3 %copy-start = (f32[8,4096]{1,0:T(8,128)S(1)}, f32[8,4096]{1,0:T(8,128)}, u32[]{:S(2)}) copy-start(f32[8,4096]{1,0:T(8,128)} %scales.1) | copy-start | bytes 393220
  38.5 3.6 %collective-permute-start = (f32[136,128]{1,0:T(8,128)S(1)}, f32[136,128]{1,0:T(8,128)S(1)}, u32[]{:S(2)}, u32[]{:S(2)}) collective-permute-start(f32[136,128]{1,0:T(8,128)S(1)} %get-tuple-element.11), channel_id=1, source_target_pairs={{0,16},{16,0},{1,17},{17,1},{2,18},{18,2},{3,19},{19,3},{4,20},{20... | collective-permute-start | bytes 208904 | tf_op jit(solution)/shard_map/ppermute | solution.py:219
  42.0 6.7 %collective-permute-start.1 = (f32[136,128]{1,0:T(8,128)S(1)}, f32[136,128]{1,0:T(8,128)S(1)}, u32[]{:S(2)}, u32[]{:S(2)}) collective-permute-start(f32[136,128]{1,0:T(8,128)S(1)} %add.4.a), channel_id=1, source_target_pairs={{0,96},{96,0},{32,192},{192,32},{64,160},{160,64},{128,224},{224,1... | collective-permute-start | bytes 208904 | tf_op jit(solution)/shard_map/ppermute | solution.py:222
  48.7 5.7 %collective-permute-start.2 = (f32[136,128]{1,0:T(8,128)S(1)}, f32[136,128]{1,0:T(8,128)S(1)}, u32[]{:S(2)}, u32[]{:S(2)}) collective-permute-start(f32[136,128]{1,0:T(8,128)S(1)} %add.5.a), channel_id=1, source_target_pairs={{32,64},{64,32},{96,128},{128,96},{160,192},{192,160},{224,0},{0,2... | collective-permute-start | bytes 208904 | tf_op jit(solution)/shard_map/ppermute | solution.py:222
  54.5 3.2 %collective-permute-start.3 = (f32[136,128]{1,0:T(8,128)S(1)}, f32[136,128]{1,0:T(8,128)S(1)}, u32[]{:S(2)}, u32[]{:S(2)}) collective-permute-start(f32[136,128]{1,0:T(8,128)S(1)} %add.6.a), channel_id=1, source_target_pairs={{0,32},{32,0},{64,96},{96,64},{128,160},{160,128},{192,224},{224,1... | collective-permute-start | bytes 208904 | tf_op jit(solution)/shard_map/ppermute | solution.py:222
  57.7 5.5 %collective-permute-start.4 = (f32[136,128]{1,0:T(8,128)S(1)}, f32[136,128]{1,0:T(8,128)S(1)}, u32[]{:S(2)}, u32[]{:S(2)}) collective-permute-start(f32[136,128]{1,0:T(8,128)S(1)} %add.7.x.mine), channel_id=1, source_target_pairs={{0,16},{16,0},{1,17},{17,1},{2,18},{18,2},{3,19},{19,3},{4,20},{20... | collective-permute-start | bytes 208904 | tf_op jit(solution)/shard_map/ppermute | solution.py:223

commit v5 on v4

--- a/solution.py
+++ b/solution.py
@@ -11,12 +11,6 @@
 HBM = pl.BlockSpec(memory_space=pltpu.HBM)
 VM = pl.BlockSpec(memory_space=pltpu.VMEM)
 CHUNKS = 4
-PAIRS = {
-    "a": ((0, 1), (2, 3), (4, 5), (6, 7)),
-    "b": ((1, 2), (3, 4), (5, 6), (7, 0)),
-    "c": ((0, 3), (1, 6), (2, 5), (4, 7)),
-}
-ORDER = "cba"
 AHEAD = 2
 PANEL = 8
 LANES = 128
@@ -77,6 +71,10 @@
     out[...] = a[...] + b[...]
 
 
+def add_four_kernel(a, b, c, d, out):
+    out[...] = (a[...] + b[...]) + (c[...] + d[...])
+
+
 def project_kernel(pieces, scales, exposure, mine, other, both, w, acc):
     groups, size, width = pieces.shape
     blocks = scales.shape[0]
@@ -121,9 +119,11 @@
     other[half * size :] = packed
 
 
-def solve_kernel(factor, x, pieces, lower, basis):
+def solve_kernel(factor, mine, across, beside, corner, pieces, basis, projected):
     groups, size, width = pieces.shape
     rows = LANES // size
+    x = mine[...] + across[...]
+    y = beside[...] + corner[...]
     packed = x[x.shape[0] - size // rows :, :]
     gram = jnp.concatenate([packed[:, i * size : (i + 1) * size] for i in range(rows)], axis=0)
     row = lax.broadcasted_iota(jnp.int32, (size, LANES), 0)
@@ -143,29 +143,21 @@
             for m in range(k + 1, PANEL):
                 cols[m] = cols[m] - scaled * cols[m][j : j + 1, :]
     linv = inv[:, size : 2 * size]
-    lower[...] = linv
-    hi, lo = split2(linv * factor)
-    lhs = jnp.concatenate([hi, lo, hi, lo], axis=1)
+    lhs = jnp.concatenate(split2(linv) * 2, axis=1)
+    half = projected.shape[1] // LANES // 2
+    is_first = lax.axis_index("core") == 0
+    low = jnp.concatenate([x[b * size : (b + 1) * size] for b in range(half)], axis=1)
+    high = jnp.concatenate([y[b * size : (b + 1) * size] for b in range(half)], axis=1)
+    low, high = jnp.where(is_first, low, high), jnp.where(is_first, high, low)
+    for part, at in ((low, 0), (high, half * LANES)):
+        shi, slo = split2(part)
+        rhs = jnp.concatenate([shi, shi, slo, slo], axis=0)
+        projected[:, at : at + half * LANES] = jnp.dot(lhs, rhs, preferred_element_type=F32)
+    lhs = jnp.concatenate(split2(linv * factor) * 2, axis=1)
     for g in range(groups):
         shi, slo = split2(pieces[g])
         rhs = jnp.concatenate([shi, shi, slo, slo], axis=0)
         basis[:, g * width : (g + 1) * width] = jnp.dot(lhs, rhs, preferred_element_type=F32)
-
-
-def finish_kernel(lower, mine, other, out):
-    size, cols = out.shape
-    half = cols // LANES // 2
-    is_first = lax.axis_index("core") == 0
-    hi, lo = split2(lower[...])
-    lhs = jnp.concatenate([hi, lo, hi, lo], axis=1)
-    low, high = [], []
-    for b in range(half):
-        m, o = mine[b * size : (b + 1) * size], other[b * size : (b + 1) * size]
-        low.append(jnp.where(is_first, m, o))
-        high.append(jnp.where(is_first, o, m))
-    shi, slo = split2(jnp.concatenate(low + high, axis=1))
-    rhs = jnp.concatenate([shi, shi, slo, slo], axis=0)
-    out[...] = jnp.dot(lhs, rhs, preferred_element_type=F32)
 
 
 def call(kernel, name, out_shape, in_specs, limit=8, scratch=()):
@@ -215,19 +207,26 @@
         ],
     )(pieces, scales, held)
 
-    add = call(add_kernel, "add", shape((tall, LANES), F32), [VM, VM])
+    def add(*xs):
+        kernel = add_kernel if len(xs) == 2 else add_four_kernel
+        return call(kernel, "add", shape((tall, LANES), F32), [VM] * len(xs))(*xs)
+
+    def swapped(x, swaps):
+        return lax.ppermute(x, "z", [p for i, j in swaps for p in ((i, j), (j, i))])
+
     total = add(mine, lax.ppermute(other, "core", swap))
-    for step in ORDER:
-        both_ways = [p for i, j in PAIRS[step] for p in ((i, j), (j, i))]
-        total = add(total, lax.ppermute(total, "z", both_ways))
-    total_other = lax.ppermute(total, "core", swap)
-    lower, basis = call(
+    total = add(total, swapped(total, ((0, 3), (1, 6), (2, 5), (4, 7))))
+    total = add(total, swapped(total, ((1, 2), (3, 4), (5, 6), (7, 0))))
+    links = [p for i, j in ((0, 1), (2, 3), (4, 5), (6, 7)) for p in ((i, j), (j, i))]
+    across = lax.ppermute(total, "z", links)
+    beside = lax.ppermute(total, "core", swap)
+    corner = lax.ppermute(
+        total, ("z", "core"), [(2 * i + c, 2 * j + 1 - c) for i, j in links for c in range(2)]
+    )
+    basis, projected = call(
         functools.partial(solve_kernel, float(total_paths) ** 0.5), "solve",
-        (shape((size, size), F32), shape((size, rows), F32)), [VM, VM],
-    )(total, pieces)
-    projected = call(finish_kernel, "finish", shape((size, cols), F32), [VM, VM, VM])(
-        lower, total, total_other
-    )
+        (shape((size, rows), F32), shape((size, cols), F32)), [VM] * 5,
+    )(total, across, beside, corner, pieces)
     return (basis, projected)
 
 

time: 64.3 us -> 63.5 us (0.988)
  Pallas kernels: 9.61 us -> 8.76 us
    pallas_call x5 -> x3, Pallas kernels: 0.92 us -> 0.03 us  [add(): return call(kernel, 'add', shape((tall, LANES), F32), [VM] * len(xs))(*xs)]
    ppermute x4 -> x5, waiting for transfers between devices: 6.72 us -> 7.05 us  [the longest x2 3.97 us: swapped(): return lax.ppermute(x, 'z', [p for i, j in swaps for p in ((i, j), (j, i))])]
    ppermute x4 -> x5, starting transfers between devices: 12.5 us -> 12.2 us  [the longest x2 8.43 us: swapped(): return lax.ppermute(x, 'z', [p for i, j in swaps for p in ((i, j), (j, i))])]
  transfers between devices with their start and end apart: 5 -> 6, of which waited for: 4 -> 5; matrix products, arithmetic and copies ran while one was open for 0% -> 0% of each run, Pallas kernels for 3% -> 0%
where the time goes in v5:
time: 63.5 us; the launch traced here: 63.3 us
  blocking collectives  31 us (49%)
  starting transfers between devices  14.9 us (23%)
  Pallas kernels  8.76 us (14%)
  waiting for transfers between devices  7.96 us (13%)
  between operations  0.68 us (1%)
    all_to_all x1, blocking collectives, per_device(): got = lax.all_to_all(partial, ('y', 'x'), 0, 0)  17.9 us
    all_to_all x1, blocking collectives, per_device(): pieces = lax.all_to_all(spread, ('y', 'x'), 0, 0)  13.1 us
    ppermute x2, starting transfers between devices, swapped(): return lax.ppermute(x, 'z', [p for i, j in swaps for p in ((i, j), (j, i))])  8.43 us
    pallas_call x1, Pallas kernels, per_device(): call(sketch_kernel, 'sketch', (shape((n_col, size, width), F32), pltpu.VM...  5.27 us
    ppermute x2, waiting for transfers between devices, swapped(): return lax.ppermute(x, 'z', [p for i, j in swaps for p in ((i, j), (j, i))])  3.97 us
    ppermute x1, starting transfers between devices, per_device(): total = add(mine, lax.ppermute(other, 'core', swap))  2.66 us
    ppermute x1, starting transfers between devices, per_device(): lax.ppermute(total, ('z', 'core'), [(2 * i + c, 2 * j + 1 - c) for i, j i...  2.5 us
    ppermute x1, waiting for transfers between devices, per_device(): across = lax.ppermute(total, 'z', links)  2.4 us
  transfers between devices with their start and end apart: 6, of which 5 were waited for; matrix products, arithmetic and copies ran while one was open for 0% of the time, Pallas kernels for 0%

profile of v5, /device:TPU:1, one launch (start us, length us, event | category | flops | bytes accessed | tf_op | source)
XLA Modules:
  0.0 63.3 jit_solution(13506437780981792950)
XLA Ops:
  0.6 0.0 copy-start
  0.6 5.3 %sketch.1 = (f32[16,32,256]{2,1,0:T(8,128)S(1)}, bf16[4096,1024]{1,0:T(8,128)(2,1)S(1)}) custom-call(bf16[32,1024]{1,0:T(8,128)(2,1)} %sketch_hbm.1, f32[8,4096]{1,0:T(8,128)} %scales.1, bf16[4096,1024]{1,0:T(8,128)(2,1)} %exposure.1), custom_call_target="tpu_custom_call" | custom-call | tf_op jit(solution)/shard_map/sketch/pallas_call | solution.py:190
  5.9 17.9 %all_to_all.10.x = f32[16,32,256]{2,1,0:T(8,128)S(1)} all-to-all(f32[16,32,256]{2,1,0:T(8,128)S(1)} %get-tuple-element.6), channel_id=1, replica_groups=mesh['z'=8,'core'=2,'y'=4,'x'=4] {'y','x'}, dimensions={0} | all-to-all | bytes 1048576 | tf_op jit(solution)/shard_map/all_to_all | solution.py:198
  23.8 0.1 sum_parts.1
  23.9 13.1 %all_to_all.11.pieces = f32[16,32,256]{2,1,0:T(8,128)S(1)} all-to-all(f32[16,32,256]{2,1,0:T(8,128)S(1)} %sum_parts.1), channel_id=1, replica_groups=mesh['z'=8,'core'=2,'y'=4,'x'=4] {'y','x'}, dimensions={0} | all-to-all | bytes 1048576 | tf_op jit(solution)/shard_map/all_to_all | solution.py:200
  37.0 0.0 copy-done
  37.0 1.5 %project.1 = (f32[136,128]{1,0:T(8,128)S(1)}, f32[136,128]{1,0:T(8,128)S(1)}) custom-call(f32[16,32,256]{2,1,0:T(8,128)S(1)} %all_to_all.11.pieces, f32[8,4096]{1,0:T(8,128)S(1)} %copy-done, bf16[4096,1024]{1,0:T(8,128)(2,1)S(1)} %get-tuple-element.7.exposure), custom_call_target="tpu_custom_call" | custom-call | tf_op jit(solution)/shard_map/project/pallas_call | solution.py:202
  38.5 2.7 %collective-permute-start = (f32[136,128]{1,0:T(8,128)S(1)}, f32[136,128]{1,0:T(8,128)S(1)}, u32[]{:S(2)}, u32[]{:S(2)}) collective-permute-start(f32[136,128]{1,0:T(8,128)S(1)} %get-tuple-element.9), channel_id=1, source_target_pairs={{0,16},{16,0},{1,17},{17,1},{2,18},{18,2},{3,19},{19,3},{4,20},{20... | collective-permute-start | bytes 208904 | tf_op jit(solution)/shard_map/ppermute | solution.py:217
  41.1 0.9 %collective-permute-done.b = f32[136,128]{1,0:T(8,128)S(1)} collective-permute-done((f32[136,128]{1,0:T(8,128)S(1)}, f32[136,128]{1,0:T(8,128)S(1)}, u32[]{:S(2)}, u32[]{:S(2)}) %collective-permute-start) | collective-permute-done | bytes 69664 | tf_op jit(solution)/shard_map/ppermute | solution.py:217
  42.0 4.4 %collective-permute-start.1 = (f32[136,128]{1,0:T(8,128)S(1)}, f32[136,128]{1,0:T(8,128)S(1)}, u32[]{:S(2)}, u32[]{:S(2)}) collective-permute-start(f32[136,128]{1,0:T(8,128)S(1)} %add.3.a), channel_id=1, source_target_pairs={{0,96},{96,0},{32,192},{192,32},{64,160},{160,64},{128,224},{224,1... | collective-permute-start | bytes 208904 | tf_op jit(solution)/shard_map/ppermute | solution.py:215
  46.5 2.3 %collective-permute-done.1.b = f32[136,128]{1,0:T(8,128)S(1)} collective-permute-done((f32[136,128]{1,0:T(8,128)S(1)}, f32[136,128]{1,0:T(8,128)S(1)}, u32[]{:S(2)}, u32[]{:S(2)}) %collective-permute-start.1) | collective-permute-done | bytes 69664 | tf_op jit(solution)/shard_map/ppermute | solution.py:215
  48.7 4.0 %collective-permute-start.2 = (f32[136,128]{1,0:T(8,128)S(1)}, f32[136,128]{1,0:T(8,128)S(1)}, u32[]{:S(2)}, u32[]{:S(2)}) collective-permute-start(f32[136,128]{1,0:T(8,128)S(1)} %add.4.a), channel_id=1, source_target_pairs={{32,64},{64,32},{96,128},{128,96},{160,192},{192,160},{224,0},{0,2... | collective-permute-start | bytes 208904 | tf_op jit(solution)/shard_map/ppermute | solution.py:215
  52.8 1.7 %collective-permute-done.2.b = f32[136,128]{1,0:T(8,128)S(1)} collective-permute-done((f32[136,128]{1,0:T(8,128)S(1)}, f32[136,128]{1,0:T(8,128)S(1)}, u32[]{:S(2)}, u32[]{:S(2)}) %collective-permute-start.2) | collective-permute-done | bytes 69664 | tf_op jit(solution)/shard_map/ppermute | solution.py:215
  54.5 2.5 %collective-permute-start.5 = (f32[136,128]{1,0:T(8,128)S(1)}, f32[136,128]{1,0:T(8,128)S(1)}, u32[]{:S(2)}, u32[]{:S(2)}) collective-permute-start(f32[136,128]{1,0:T(8,128)S(1)} %add.5.mine), channel_id=1, source_target_pairs={{0,48},{16,32},{32,16},{48,0},{64,112},{80,96},{96,80},{112,64},{1... | collective-permute-start | bytes 208904 | tf_op jit(solution)/shard_map/ppermute | solution.py:223
  57.0 0.1 collective-permute-start.4
  57.0 1.3 %collective-permute-start.3 = (f32[136,128]{1,0:T(8,128)S(1)}, f32[136,128]{1,0:T(8,128)S(1)}, u32[]{:S(2)}, u32[]{:S(2)}) collective-permute-start(f32[136,128]{1,0:T(8,128)S(1)} %add.5.mine), channel_id=1, source_target_pairs={{0,32},{32,0},{64,96},{96,64},{128,160},{160,128},{192,224},{224,1... | collective-permute-start | bytes 208904 | tf_op jit(solution)/shard_map/ppermute | solution.py:221
  58.3 0.7 %collective-permute-done.5.corner = f32[136,128]{1,0:T(8,128)S(1)} collective-permute-done((f32[136,128]{1,0:T(8,128)S(1)}, f32[136,128]{1,0:T(8,128)S(1)}, u32[]{:S(2)}, u32[]{:S(2)}) %collective-permute-start.5) | collective-permute-done | bytes 69664 | tf_op jit(solution)/shard_map/ppermute | solution.py:223
  59.0 0.0 collective-permute-done.4.beside
  59.0 2.4 %collective-permute-done.3.across = f32[136,128]{1,0:T(8,128)S(1)} collective-permute-done((f32[136,128]{1,0:T(8,128)S(1)}, f32[136,128]{1,0:T(8,128)S(1)}, u32[]{:S(2)}, u32[]{:S(2)}) %collective-permute-start.3) | collective-permute-done | bytes 69664 | tf_op jit(solution)/shard_map/ppermute | solution.py:221
  61.4 1.9 %solve.1 = (f32[32,4096]{1,0:T(8,128)}, f32[32,1024]{1,0:T(8,128)}) custom-call(f32[136,128]{1,0:T(8,128)S(1)} %add.5.mine, f32[136,128]{1,0:T(8,128)S(1)} %collective-permute-done.3.across, f32[136,128]{1,0:T(8,128)S(1)} %collective-permute-done.4.beside, f32[136,128]{1,0:T(8,128)S(1)} %collective-permute-done.5.corner, f32[16,32,256]{2,1,0:T(8,128)S(1)} %all_to_all.11.pieces), custom_call_target="tpu_custom_call" | custom-call | tf_op jit(solution)/shard_map/solve/pallas_call | solution.py:226
  (3 shorter events, 0.0 us)
Async XLA Ops:
  0.6 36.3 %copy-start = (f32[8,4096]{1,0:T(8,128)S(1)}, f32[8,4096]{1,0:T(8,128)}, u32[]{:S(2)}) copy-start(f32[8,4096]{1,0:T(8,128)} %scales.1) | copy-start | bytes 393220
  38.5 3.6 %collective-permute-start = (f32[136,128]{1,0:T(8,128)S(1)}, f32[136,128]{1,0:T(8,128)S(1)}, u32[]{:S(2)}, u32[]{:S(2)}) collective-permute-start(f32[136,128]{1,0:T(8,128)S(1)} %get-tuple-element.9), channel_id=1, source_target_pairs={{0,16},{16,0},{1,17},{17,1},{2,18},{18,2},{3,19},{19,3},{4,20},{20... | collective-permute-start | bytes 208904 | tf_op jit(solution)/shard_map/ppermute | solution.py:217
  42.0 6.7 %collective-permute-start.1 = (f32[136,128]{1,0:T(8,128)S(1)}, f32[136,128]{1,0:T(8,128)S(1)}, u32[]{:S(2)}, u32[]{:S(2)}) collective-permute-start(f32[136,128]{1,0:T(8,128)S(1)} %add.3.a), channel_id=1, source_target_pairs={{0,96},{96,0},{32,192},{192,32},{64,160},{160,64},{128,224},{224,1... | collective-permute-start | bytes 208904 | tf_op jit(solution)/shard_map/ppermute | solution.py:215
  48.7 5.7 %collective-permute-start.2 = (f32[136,128]{1,0:T(8,128)S(1)}, f32[136,128]{1,0:T(8,128)S(1)}, u32[]{:S(2)}, u32[]{:S(2)}) collective-permute-start(f32[136,128]{1,0:T(8,128)S(1)} %add.4.a), channel_id=1, source_target_pairs={{32,64},{64,32},{96,128},{128,96},{160,192},{192,160},{224,0},{0,2... | collective-permute-start | bytes 208904 | tf_op jit(solution)/shard_map/ppermute | solution.py:215
  54.5 4.5 %collective-permute-start.5 = (f32[136,128]{1,0:T(8,128)S(1)}, f32[136,128]{1,0:T(8,128)S(1)}, u32[]{:S(2)}, u32[]{:S(2)}) collective-permute-start(f32[136,128]{1,0:T(8,128)S(1)} %add.5.mine), channel_id=1, source_target_pairs={{0,48},{16,32},{32,16},{48,0},{64,112},{80,96},{96,80},{112,64},{1... | collective-permute-start | bytes 208904 | tf_op jit(solution)/shard_map/ppermute | solution.py:223
  57.0 2.0 %collective-permute-start.4 = (f32[136,128]{1,0:T(8,128)S(1)}, f32[136,128]{1,0:T(8,128)S(1)}, u32[]{:S(2)}, u32[]{:S(2)}) collective-permute-start(f32[136,128]{1,0:T(8,128)S(1)} %add.5.mine), channel_id=1, source_target_pairs={{0,16},{16,0},{1,17},{17,1},{2,18},{18,2},{3,19},{19,3},{4,20},{20... | collective-permute-start | bytes 208904 | tf_op jit(solution)/shard_map/ppermute | solution.py:222
  57.0 4.3 %collective-permute-start.3 = (f32[136,128]{1,0:T(8,128)S(1)}, f32[136,128]{1,0:T(8,128)S(1)}, u32[]{:S(2)}, u32[]{:S(2)}) collective-permute-start(f32[136,128]{1,0:T(8,128)S(1)} %add.5.mine), channel_id=1, source_target_pairs={{0,32},{32,0},{64,96},{96,64},{128,160},{160,128},{192,224},{224,1... | collective-permute-start | bytes 208904 | tf_op jit(solution)/shard_map/ppermute | solution.py:221

commit v6 on v5

--- a/solution.py
+++ b/solution.py
@@ -12,7 +12,7 @@
 VM = pl.BlockSpec(memory_space=pltpu.VMEM)
 CHUNKS = 4
 AHEAD = 2
-PANEL = 8
+PANEL = 16
 LANES = 128
 NT = (((1,), (1,)), ((), ()))
 
@@ -26,7 +26,7 @@
     return slice(b * LANES, (b + n) * LANES)
 
 
-def sketch_kernel(sketch_hbm, scales_hbm, exposure, out, held, sketch, scales, diag, sems, small):
+def sketch_kernel(sketch_hbm, scales_hbm, exposure, out, held, scales, sketch, diag, sems, small):
     size = sketch.shape[0]
     blocks = scales.shape[0]
     groups, _, width = out.shape
@@ -187,17 +187,18 @@
     shape = jax.ShapeDtypeStruct
     DMA = pltpu.SemaphoreType.DMA
 
-    partial, held = call(
-        sketch_kernel, "sketch", (shape((n_col, size, width), F32), pltpu.VMEM((rows, cols), BF)),
+    partial, held, scales = call(
+        sketch_kernel, "sketch",
+        (shape((n_col, size, width), F32), pltpu.VMEM((rows, cols), BF), pltpu.VMEM((blocks, rows), F32)),
         [HBM] * 3, 40,
         [
-            pltpu.VMEM((size, cols), BF), pltpu.VMEM((blocks, rows), F32),
+            pltpu.VMEM((size, cols), BF),
             pltpu.VMEM((blocks * size, cols), BF), DMA((CHUNKS,)), DMA((2,)),
         ],
     )(*(pltpu.with_memory_space_constraint(x, pltpu.HBM) for x in (sketch, scales, exposure)))
-    got = lax.all_to_all(partial, ("y", "x"), 0, 0)
+    got = lax.all_to_all(partial, ("x", "y"), 0, 0)
     spread = call(sum_copies_kernel, "sum_parts", shape((n_col, size, width), F32), [VM])(got)
-    pieces = lax.all_to_all(spread, ("y", "x"), 0, 0)
+    pieces = lax.all_to_all(spread, ("x", "y"), 0, 0)
 
     mine, other = call(
         project_kernel, "project", (shape((tall, LANES), F32),) * 2, [VM, VM, VM], 40,

time: 63.5 us -> 62.8 us (0.989)
  blocking collectives: 31 us -> 30.2 us
  starting transfers between devices: 14.9 us -> 15.6 us
    all_to_all x2, blocking collectives: 31 us -> 30.2 us  [the longest x1 17.7 us: per_device(): got = lax.all_to_all(partial, ('x', 'y'), 0, 0)]
    ppermute x1, starting transfers between devices: 2.66 us -> 3.32 us  [per_device(): total = add(mine, lax.ppermute(other, 'core', swap))]
where the time goes in v6:
time: 62.8 us; the launch traced here: 62.7 us
  blocking collectives  30.2 us (48%)
  starting transfers between devices  15.6 us (25%)
  Pallas kernels  8.28 us (13%)
  waiting for transfers between devices  7.96 us (13%)
  between operations  0.67 us (1%)
    all_to_all x1, blocking collectives, per_device(): got = lax.all_to_all(partial, ('x', 'y'), 0, 0)  17.7 us
    all_to_all x1, blocking collectives, per_device(): pieces = lax.all_to_all(spread, ('x', 'y'), 0, 0)  12.5 us
    ppermute x2, starting transfers between devices, swapped(): return lax.ppermute(x, 'z', [p for i, j in swaps for p in ((i, j), (j, i))])  8.44 us
    pallas_call x1, Pallas kernels, per_device(): call(sketch_kernel, 'sketch', (shape((n_col, size, width), F32), pltpu.VM...  4.92 us
    ppermute x2, waiting for transfers between devices, swapped(): return lax.ppermute(x, 'z', [p for i, j in swaps for p in ((i, j), (j, i))])  3.97 us
    ppermute x1, starting transfers between devices, per_device(): total = add(mine, lax.ppermute(other, 'core', swap))  3.32 us
    ppermute x1, starting transfers between devices, per_device(): lax.ppermute(total, ('z', 'core'), [(2 * i + c, 2 * j + 1 - c) for i, j i...  2.49 us
    ppermute x1, waiting for transfers between devices, per_device(): across = lax.ppermute(total, 'z', links)  2.41 us
  transfers between devices with their start and end apart: 6, of which 5 were waited for; matrix products, arithmetic and copies ran while one was open for 0% of the time, Pallas kernels for 0%

profile of v6, /device:TPU:1, one launch (start us, length us, event | category | flops | bytes accessed | tf_op | source)
XLA Modules:
  0.0 62.7 jit_solution(2162450709821586672)
XLA Ops:
  0.6 4.9 %sketch.1 = (f32[16,32,256]{2,1,0:T(8,128)S(1)}, bf16[4096,1024]{1,0:T(8,128)(2,1)S(1)}, f32[8,4096]{1,0:T(8,128)S(1)}) custom-call(bf16[32,1024]{1,0:T(8,128)(2,1)} %sketch_hbm.1, f32[8,4096]{1,0:T(8,128)} %scales_hbm.1, bf16[4096,1024]{1,0:T(8,128)(2,1)} %exposure.1), custom_call_target="tpu_custom_call" | custom-call | tf_op jit(solution)/shard_map/sketch/pallas_call | solution.py:190
  5.6 17.7 %all_to_all.10.x = f32[16,32,256]{2,1,0:T(8,128)S(1)} all-to-all(f32[16,32,256]{2,1,0:T(8,128)S(1)} %get-tuple-element.7), channel_id=1, replica_groups=mesh['z'=8,'core'=2,'y'=4,'x'=4] {'x','y'}, dimensions={0} | all-to-all | bytes 1048576 | tf_op jit(solution)/shard_map/all_to_all | solution.py:199
  23.2 0.1 sum_parts.1
  23.3 12.5 %all_to_all.11.pieces = f32[16,32,256]{2,1,0:T(8,128)S(1)} all-to-all(f32[16,32,256]{2,1,0:T(8,128)S(1)} %sum_parts.1), channel_id=1, replica_groups=mesh['z'=8,'core'=2,'y'=4,'x'=4] {'x','y'}, dimensions={0} | all-to-all | bytes 1048576 | tf_op jit(solution)/shard_map/all_to_all | solution.py:201
  35.8 1.5 %project.1 = (f32[136,128]{1,0:T(8,128)S(1)}, f32[136,128]{1,0:T(8,128)S(1)}) custom-call(f32[16,32,256]{2,1,0:T(8,128)S(1)} %all_to_all.11.pieces, f32[8,4096]{1,0:T(8,128)S(1)} %get-tuple-element.8.scales, bf16[4096,1024]{1,0:T(8,128)(2,1)S(1)} %get-tuple-element.9.exposure), custom_call_target="tpu_custom_call" | custom-call | tf_op jit(solution)/shard_map/project/pallas_call | solution.py:203
  37.3 3.3 %collective-permute-start = (f32[136,128]{1,0:T(8,128)S(1)}, f32[136,128]{1,0:T(8,128)S(1)}, u32[]{:S(2)}, u32[]{:S(2)}) collective-permute-start(f32[136,128]{1,0:T(8,128)S(1)} %get-tuple-element.11), channel_id=1, source_target_pairs={{0,16},{16,0},{1,17},{17,1},{2,18},{18,2},{3,19},{19,3},{4,20},{20... | collective-permute-start | bytes 208904 | tf_op jit(solution)/shard_map/ppermute | solution.py:218
  40.6 0.9 %collective-permute-done.b = f32[136,128]{1,0:T(8,128)S(1)} collective-permute-done((f32[136,128]{1,0:T(8,128)S(1)}, f32[136,128]{1,0:T(8,128)S(1)}, u32[]{:S(2)}, u32[]{:S(2)}) %collective-permute-start) | collective-permute-done | bytes 69664 | tf_op jit(solution)/shard_map/ppermute | solution.py:218
  41.5 4.4 %collective-permute-start.1 = (f32[136,128]{1,0:T(8,128)S(1)}, f32[136,128]{1,0:T(8,128)S(1)}, u32[]{:S(2)}, u32[]{:S(2)}) collective-permute-start(f32[136,128]{1,0:T(8,128)S(1)} %add.3.a), channel_id=1, source_target_pairs={{0,96},{96,0},{32,192},{192,32},{64,160},{160,64},{128,224},{224,1... | collective-permute-start | bytes 208904 | tf_op jit(solution)/shard_map/ppermute | solution.py:216
  46.0 2.3 %collective-permute-done.1.b = f32[136,128]{1,0:T(8,128)S(1)} collective-permute-done((f32[136,128]{1,0:T(8,128)S(1)}, f32[136,128]{1,0:T(8,128)S(1)}, u32[]{:S(2)}, u32[]{:S(2)}) %collective-permute-start.1) | collective-permute-done | bytes 69664 | tf_op jit(solution)/shard_map/ppermute | solution.py:216
  48.3 4.0 %collective-permute-start.2 = (f32[136,128]{1,0:T(8,128)S(1)}, f32[136,128]{1,0:T(8,128)S(1)}, u32[]{:S(2)}, u32[]{:S(2)}) collective-permute-start(f32[136,128]{1,0:T(8,128)S(1)} %add.4.a), channel_id=1, source_target_pairs={{32,64},{64,32},{96,128},{128,96},{160,192},{192,160},{224,0},{0,2... | collective-permute-start | bytes 208904 | tf_op jit(solution)/shard_map/ppermute | solution.py:216
  52.3 1.7 %collective-permute-done.2.b = f32[136,128]{1,0:T(8,128)S(1)} collective-permute-done((f32[136,128]{1,0:T(8,128)S(1)}, f32[136,128]{1,0:T(8,128)S(1)}, u32[]{:S(2)}, u32[]{:S(2)}) %collective-permute-start.2) | collective-permute-done | bytes 69664 | tf_op jit(solution)/shard_map/ppermute | solution.py:216
  54.0 2.5 %collective-permute-start.5 = (f32[136,128]{1,0:T(8,128)S(1)}, f32[136,128]{1,0:T(8,128)S(1)}, u32[]{:S(2)}, u32[]{:S(2)}) collective-permute-start(f32[136,128]{1,0:T(8,128)S(1)} %add.5.mine), channel_id=1, source_target_pairs={{0,48},{16,32},{32,16},{48,0},{64,112},{80,96},{96,80},{112,64},{1... | collective-permute-start | bytes 208904 | tf_op jit(solution)/shard_map/ppermute | solution.py:224
  56.5 0.1 collective-permute-start.4
  56.5 1.3 %collective-permute-start.3 = (f32[136,128]{1,0:T(8,128)S(1)}, f32[136,128]{1,0:T(8,128)S(1)}, u32[]{:S(2)}, u32[]{:S(2)}) collective-permute-start(f32[136,128]{1,0:T(8,128)S(1)} %add.5.mine), channel_id=1, source_target_pairs={{0,32},{32,0},{64,96},{96,64},{128,160},{160,128},{192,224},{224,1... | collective-permute-start | bytes 208904 | tf_op jit(solution)/shard_map/ppermute | solution.py:222
  57.8 0.7 %collective-permute-done.5.corner = f32[136,128]{1,0:T(8,128)S(1)} collective-permute-done((f32[136,128]{1,0:T(8,128)S(1)}, f32[136,128]{1,0:T(8,128)S(1)}, u32[]{:S(2)}, u32[]{:S(2)}) %collective-permute-start.5) | collective-permute-done | bytes 69664 | tf_op jit(solution)/shard_map/ppermute | solution.py:224
  58.5 0.0 collective-permute-done.4.beside
  58.5 2.4 %collective-permute-done.3.across = f32[136,128]{1,0:T(8,128)S(1)} collective-permute-done((f32[136,128]{1,0:T(8,128)S(1)}, f32[136,128]{1,0:T(8,128)S(1)}, u32[]{:S(2)}, u32[]{:S(2)}) %collective-permute-start.3) | collective-permute-done | bytes 69664 | tf_op jit(solution)/shard_map/ppermute | solution.py:222
  60.9 1.8 %solve.1 = (f32[32,4096]{1,0:T(8,128)}, f32[32,1024]{1,0:T(8,128)}) custom-call(f32[136,128]{1,0:T(8,128)S(1)} %add.5.mine, f32[136,128]{1,0:T(8,128)S(1)} %collective-permute-done.3.across, f32[136,128]{1,0:T(8,128)S(1)} %collective-permute-done.4.beside, f32[136,128]{1,0:T(8,128)S(1)} %collective-permute-done.5.corner, f32[16,32,256]{2,1,0:T(8,128)S(1)} %all_to_all.11.pieces), custom_call_target="tpu_custom_call" | custom-call | tf_op jit(solution)/shard_map/solve/pallas_call | solution.py:227
  (3 shorter events, 0.0 us)
Async XLA Ops:
  37.3 4.2 %collective-permute-start = (f32[136,128]{1,0:T(8,128)S(1)}, f32[136,128]{1,0:T(8,128)S(1)}, u32[]{:S(2)}, u32[]{:S(2)}) collective-permute-start(f32[136,128]{1,0:T(8,128)S(1)} %get-tuple-element.11), channel_id=1, source_target_pairs={{0,16},{16,0},{1,17},{17,1},{2,18},{18,2},{3,19},{19,3},{4,20},{20... | collective-permute-start | bytes 208904 | tf_op jit(solution)/shard_map/ppermute | solution.py:218
  41.5 6.7 %collective-permute-start.1 = (f32[136,128]{1,0:T(8,128)S(1)}, f32[136,128]{1,0:T(8,128)S(1)}, u32[]{:S(2)}, u32[]{:S(2)}) collective-permute-start(f32[136,128]{1,0:T(8,128)S(1)} %add.3.a), channel_id=1, source_target_pairs={{0,96},{96,0},{32,192},{192,32},{64,160},{160,64},{128,224},{224,1... | collective-permute-start | bytes 208904 | tf_op jit(solution)/shard_map/ppermute | solution.py:216
  48.3 5.7 %collective-permute-start.2 = (f32[136,128]{1,0:T(8,128)S(1)}, f32[136,128]{1,0:T(8,128)S(1)}, u32[]{:S(2)}, u32[]{:S(2)}) collective-permute-start(f32[136,128]{1,0:T(8,128)S(1)} %add.4.a), channel_id=1, source_target_pairs={{32,64},{64,32},{96,128},{128,96},{160,192},{192,160},{224,0},{0,2... | collective-permute-start | bytes 208904 | tf_op jit(solution)/shard_map/ppermute | solution.py:216
  54.0 4.5 %collective-permute-start.5 = (f32[136,128]{1,0:T(8,128)S(1)}, f32[136,128]{1,0:T(8,128)S(1)}, u32[]{:S(2)}, u32[]{:S(2)}) collective-permute-start(f32[136,128]{1,0:T(8,128)S(1)} %add.5.mine), channel_id=1, source_target_pairs={{0,48},{16,32},{32,16},{48,0},{64,112},{80,96},{96,80},{112,64},{1... | collective-permute-start | bytes 208904 | tf_op jit(solution)/shard_map/ppermute | solution.py:224
  56.5 2.0 %collective-permute-start.4 = (f32[136,128]{1,0:T(8,128)S(1)}, f32[136,128]{1,0:T(8,128)S(1)}, u32[]{:S(2)}, u32[]{:S(2)}) collective-permute-start(f32[136,128]{1,0:T(8,128)S(1)} %add.5.mine), channel_id=1, source_target_pairs={{0,16},{16,0},{1,17},{17,1},{2,18},{18,2},{3,19},{19,3},{4,20},{20... | collective-permute-start | bytes 208904 | tf_op jit(solution)/shard_map/ppermute | solution.py:223
  56.5 4.3 %collective-permute-start.3 = (f32[136,128]{1,0:T(8,128)S(1)}, f32[136,128]{1,0:T(8,128)S(1)}, u32[]{:S(2)}, u32[]{:S(2)}) collective-permute-start(f32[136,128]{1,0:T(8,128)S(1)} %add.5.mine), channel_id=1, source_target_pairs={{0,32},{32,0},{64,96},{96,64},{128,160},{160,128},{192,224},{224,1... | collective-permute-start | bytes 208904 | tf_op jit(solution)/shard_map/ppermute | solution.py:222

commit v7 on v6

--- a/solution.py
+++ b/solution.py
@@ -14,6 +14,7 @@
 AHEAD = 2
 PANEL = 16
 LANES = 128
+GROUPS = [[4 * (j % 4) + j // 4 for j in range(16)], [31 - j for j in range(16)]]
 NT = (((1,), (1,)), ((), ()))
 
 
@@ -196,9 +197,9 @@
             pltpu.VMEM((blocks * size, cols), BF), DMA((CHUNKS,)), DMA((2,)),
         ],
     )(*(pltpu.with_memory_space_constraint(x, pltpu.HBM) for x in (sketch, scales, exposure)))
-    got = lax.all_to_all(partial, ("x", "y"), 0, 0)
+    got = lax.all_to_all(partial, ("core", "y", "x"), 0, 0, axis_index_groups=GROUPS)
     spread = call(sum_copies_kernel, "sum_parts", shape((n_col, size, width), F32), [VM])(got)
-    pieces = lax.all_to_all(spread, ("x", "y"), 0, 0)
+    pieces = lax.all_to_all(spread, ("core", "y", "x"), 0, 0, axis_index_groups=GROUPS)
 
     mine, other = call(
         project_kernel, "project", (shape((tall, LANES), F32),) * 2, [VM, VM, VM], 40,

time: 62.8 us -> 61.9 us (0.986)
  blocking collectives: 30.2 us -> 29.2 us
    all_to_all x2, blocking collectives: 30.2 us -> 29.2 us  [the longest x1 15.1 us: per_device(): lax.all_to_all(partial, ('core', 'y', 'x'), 0, 0, axis_index_groups=GROUPS)]
where the time goes in v7:
time: 61.9 us; the launch traced here: 61.8 us
  blocking collectives  29.2 us (47%)
  starting transfers between devices  15.6 us (25%)
  Pallas kernels  8.28 us (13%)
  waiting for transfers between devices  7.97 us (13%)
  between operations  0.67 us (1%)
    all_to_all x1, blocking collectives, per_device(): lax.all_to_all(partial, ('core', 'y', 'x'), 0, 0, axis_index_groups=GROUPS)  15.1 us
    all_to_all x1, blocking collectives, per_device(): lax.all_to_all(spread, ('core', 'y', 'x'), 0, 0, axis_index_groups=GROUPS)  14.2 us
    ppermute x2, starting transfers between devices, swapped(): return lax.ppermute(x, 'z', [p for i, j in swaps for p in ((i, j), (j, i))])  8.44 us
    pallas_call x1, Pallas kernels, per_device(): call(sketch_kernel, 'sketch', (shape((n_col, size, width), F32), pltpu.VM...  4.92 us
    ppermute x2, waiting for transfers between devices, swapped(): return lax.ppermute(x, 'z', [p for i, j in swaps for p in ((i, j), (j, i))])  3.97 us
    ppermute x1, starting transfers between devices, per_device(): total = add(mine, lax.ppermute(other, 'core', swap))  3.33 us
    ppermute x1, starting transfers between devices, per_device(): lax.ppermute(total, ('z', 'core'), [(2 * i + c, 2 * j + 1 - c) for i, j i...  2.48 us
    ppermute x1, waiting for transfers between devices, per_device(): across = lax.ppermute(total, 'z', links)  2.43 us
  transfers between devices with their start and end apart: 6, of which 5 were waited for; matrix products, arithmetic and copies ran while one was open for 0% of the time, Pallas kernels for 0%

profile of v7, /device:TPU:1, one launch (start us, length us, event | category | flops | bytes accessed | tf_op | source)
XLA Modules:
  0.0 61.8 jit_solution(14440019729199762643)
XLA Ops:
  0.6 4.9 %sketch.1 = (f32[16,32,256]{2,1,0:T(8,128)S(1)}, bf16[4096,1024]{1,0:T(8,128)(2,1)S(1)}, f32[8,4096]{1,0:T(8,128)S(1)}) custom-call(bf16[32,1024]{1,0:T(8,128)(2,1)} %sketch_hbm.1, f32[8,4096]{1,0:T(8,128)} %scales_hbm.1, bf16[4096,1024]{1,0:T(8,128)(2,1)} %exposure.1), custom_call_target="tpu_custom_call" | custom-call | tf_op jit(solution)/shard_map/sketch/pallas_call | solution.py:191
  5.6 15.1 %all_to_all.10.x = f32[16,32,256]{2,1,0:T(8,128)S(1)} all-to-all(f32[16,32,256]{2,1,0:T(8,128)S(1)} %get-tuple-element.7), channel_id=1, replica_groups={{0,4,8,12,1,5,9,13,2,6,10,14,3,7,11,15},{31,30,29,28,27,26,25,24,23,22,..., dimensions={0} | all-to-all | bytes 1048576 | tf_op jit(solution)/shard_map/all_to_all | solution.py:200
  20.6 0.1 sum_parts.1
  20.7 14.2 %all_to_all.11.pieces = f32[16,32,256]{2,1,0:T(8,128)S(1)} all-to-all(f32[16,32,256]{2,1,0:T(8,128)S(1)} %sum_parts.1), channel_id=1, replica_groups={{0,4,8,12,1,5,9,13,2,6,10,14,3,7,11,15},{31,30,29,28,27,26,25,24,23,22,..., dimensions={0} | all-to-all | bytes 1048576 | tf_op jit(solution)/shard_map/all_to_all | solution.py:202
  34.9 1.5 %project.1 = (f32[136,128]{1,0:T(8,128)S(1)}, f32[136,128]{1,0:T(8,128)S(1)}) custom-call(f32[16,32,256]{2,1,0:T(8,128)S(1)} %all_to_all.11.pieces, f32[8,4096]{1,0:T(8,128)S(1)} %get-tuple-element.8.scales, bf16[4096,1024]{1,0:T(8,128)(2,1)S(1)} %get-tuple-element.9.exposure), custom_call_target="tpu_custom_call" | custom-call | tf_op jit(solution)/shard_map/project/pallas_call | solution.py:204
  36.4 3.3 %collective-permute-start = (f32[136,128]{1,0:T(8,128)S(1)}, f32[136,128]{1,0:T(8,128)S(1)}, u32[]{:S(2)}, u32[]{:S(2)}) collective-permute-start(f32[136,128]{1,0:T(8,128)S(1)} %get-tuple-element.11), channel_id=1, source_target_pairs={{0,16},{16,0},{1,17},{17,1},{2,18},{18,2},{3,19},{19,3},{4,20},{20... | collective-permute-start | bytes 208904 | tf_op jit(solution)/shard_map/ppermute | solution.py:219
  39.7 0.9 %collective-permute-done.b = f32[136,128]{1,0:T(8,128)S(1)} collective-permute-done((f32[136,128]{1,0:T(8,128)S(1)}, f32[136,128]{1,0:T(8,128)S(1)}, u32[]{:S(2)}, u32[]{:S(2)}) %collective-permute-start) | collective-permute-done | bytes 69664 | tf_op jit(solution)/shard_map/ppermute | solution.py:219
  40.6 4.4 %collective-permute-start.1 = (f32[136,128]{1,0:T(8,128)S(1)}, f32[136,128]{1,0:T(8,128)S(1)}, u32[]{:S(2)}, u32[]{:S(2)}) collective-permute-start(f32[136,128]{1,0:T(8,128)S(1)} %add.3.a), channel_id=1, source_target_pairs={{0,96},{96,0},{32,192},{192,32},{64,160},{160,64},{128,224},{224,1... | collective-permute-start | bytes 208904 | tf_op jit(solution)/shard_map/ppermute | solution.py:217
  45.0 2.3 %collective-permute-done.1.b = f32[136,128]{1,0:T(8,128)S(1)} collective-permute-done((f32[136,128]{1,0:T(8,128)S(1)}, f32[136,128]{1,0:T(8,128)S(1)}, u32[]{:S(2)}, u32[]{:S(2)}) %collective-permute-start.1) | collective-permute-done | bytes 69664 | tf_op jit(solution)/shard_map/ppermute | solution.py:217
  47.3 4.0 %collective-permute-start.2 = (f32[136,128]{1,0:T(8,128)S(1)}, f32[136,128]{1,0:T(8,128)S(1)}, u32[]{:S(2)}, u32[]{:S(2)}) collective-permute-start(f32[136,128]{1,0:T(8,128)S(1)} %add.4.a), channel_id=1, source_target_pairs={{32,64},{64,32},{96,128},{128,96},{160,192},{192,160},{224,0},{0,2... | collective-permute-start | bytes 208904 | tf_op jit(solution)/shard_map/ppermute | solution.py:217
  51.3 1.7 %collective-permute-done.2.b = f32[136,128]{1,0:T(8,128)S(1)} collective-permute-done((f32[136,128]{1,0:T(8,128)S(1)}, f32[136,128]{1,0:T(8,128)S(1)}, u32[]{:S(2)}, u32[]{:S(2)}) %collective-permute-start.2) | collective-permute-done | bytes 69664 | tf_op jit(solution)/shard_map/ppermute | solution.py:217
  53.0 2.5 %collective-permute-start.5 = (f32[136,128]{1,0:T(8,128)S(1)}, f32[136,128]{1,0:T(8,128)S(1)}, u32[]{:S(2)}, u32[]{:S(2)}) collective-permute-start(f32[136,128]{1,0:T(8,128)S(1)} %add.5.mine), channel_id=1, source_target_pairs={{0,48},{16,32},{32,16},{48,0},{64,112},{80,96},{96,80},{112,64},{1... | collective-permute-start | bytes 208904 | tf_op jit(solution)/shard_map/ppermute | solution.py:225
  55.5 0.1 collective-permute-start.4
  55.6 1.3 %collective-permute-start.3 = (f32[136,128]{1,0:T(8,128)S(1)}, f32[136,128]{1,0:T(8,128)S(1)}, u32[]{:S(2)}, u32[]{:S(2)}) collective-permute-start(f32[136,128]{1,0:T(8,128)S(1)} %add.5.mine), channel_id=1, source_target_pairs={{0,32},{32,0},{64,96},{96,64},{128,160},{160,128},{192,224},{224,1... | collective-permute-start | bytes 208904 | tf_op jit(solution)/shard_map/ppermute | solution.py:223
  56.9 0.7 %collective-permute-done.5.corner = f32[136,128]{1,0:T(8,128)S(1)} collective-permute-done((f32[136,128]{1,0:T(8,128)S(1)}, f32[136,128]{1,0:T(8,128)S(1)}, u32[]{:S(2)}, u32[]{:S(2)}) %collective-permute-start.5) | collective-permute-done | bytes 69664 | tf_op jit(solution)/shard_map/ppermute | solution.py:225
  57.5 0.0 collective-permute-done.4.beside
  57.5 2.4 %collective-permute-done.3.across = f32[136,128]{1,0:T(8,128)S(1)} collective-permute-done((f32[136,128]{1,0:T(8,128)S(1)}, f32[136,128]{1,0:T(8,128)S(1)}, u32[]{:S(2)}, u32[]{:S(2)}) %collective-permute-start.3) | collective-permute-done | bytes 69664 | tf_op jit(solution)/shard_map/ppermute | solution.py:223
  59.9 1.8 %solve.1 = (f32[32,4096]{1,0:T(8,128)}, f32[32,1024]{1,0:T(8,128)}) custom-call(f32[136,128]{1,0:T(8,128)S(1)} %add.5.mine, f32[136,128]{1,0:T(8,128)S(1)} %collective-permute-done.3.across, f32[136,128]{1,0:T(8,128)S(1)} %collective-permute-done.4.beside, f32[136,128]{1,0:T(8,128)S(1)} %collective-permute-done.5.corner, f32[16,32,256]{2,1,0:T(8,128)S(1)} %all_to_all.11.pieces), custom_call_target="tpu_custom_call" | custom-call | tf_op jit(solution)/shard_map/solve/pallas_call | solution.py:228
  (3 shorter events, 0.0 us)
Async XLA Ops:
  36.4 4.2 %collective-permute-start = (f32[136,128]{1,0:T(8,128)S(1)}, f32[136,128]{1,0:T(8,128)S(1)}, u32[]{:S(2)}, u32[]{:S(2)}) collective-permute-start(f32[136,128]{1,0:T(8,128)S(1)} %get-tuple-element.11), channel_id=1, source_target_pairs={{0,16},{16,0},{1,17},{17,1},{2,18},{18,2},{3,19},{19,3},{4,20},{20... | collective-permute-start | bytes 208904 | tf_op jit(solution)/shard_map/ppermute | solution.py:219
  40.6 6.7 %collective-permute-start.1 = (f32[136,128]{1,0:T(8,128)S(1)}, f32[136,128]{1,0:T(8,128)S(1)}, u32[]{:S(2)}, u32[]{:S(2)}) collective-permute-start(f32[136,128]{1,0:T(8,128)S(1)} %add.3.a), channel_id=1, source_target_pairs={{0,96},{96,0},{32,192},{192,32},{64,160},{160,64},{128,224},{224,1... | collective-permute-start | bytes 208904 | tf_op jit(solution)/shard_map/ppermute | solution.py:217
  47.3 5.7 %collective-permute-start.2 = (f32[136,128]{1,0:T(8,128)S(1)}, f32[136,128]{1,0:T(8,128)S(1)}, u32[]{:S(2)}, u32[]{:S(2)}) collective-permute-start(f32[136,128]{1,0:T(8,128)S(1)} %add.4.a), channel_id=1, source_target_pairs={{32,64},{64,32},{96,128},{128,96},{160,192},{192,160},{224,0},{0,2... | collective-permute-start | bytes 208904 | tf_op jit(solution)/shard_map/ppermute | solution.py:217
  53.0 4.5 %collective-permute-start.5 = (f32[136,128]{1,0:T(8,128)S(1)}, f32[136,128]{1,0:T(8,128)S(1)}, u32[]{:S(2)}, u32[]{:S(2)}) collective-permute-start(f32[136,128]{1,0:T(8,128)S(1)} %add.5.mine), channel_id=1, source_target_pairs={{0,48},{16,32},{32,16},{48,0},{64,112},{80,96},{96,80},{112,64},{1... | collective-permute-start | bytes 208904 | tf_op jit(solution)/shard_map/ppermute | solution.py:225
  55.5 2.0 %collective-permute-start.4 = (f32[136,128]{1,0:T(8,128)S(1)}, f32[136,128]{1,0:T(8,128)S(1)}, u32[]{:S(2)}, u32[]{:S(2)}) collective-permute-start(f32[136,128]{1,0:T(8,128)S(1)} %add.5.mine), channel_id=1, source_target_pairs={{0,16},{16,0},{1,17},{17,1},{2,18},{18,2},{3,19},{19,3},{4,20},{20... | collective-permute-start | bytes 208904 | tf_op jit(solution)/shard_map/ppermute | solution.py:224
  55.6 4.4 %collective-permute-start.3 = (f32[136,128]{1,0:T(8,128)S(1)}, f32[136,128]{1,0:T(8,128)S(1)}, u32[]{:S(2)}, u32[]{:S(2)}) collective-permute-start(f32[136,128]{1,0:T(8,128)S(1)} %add.5.mine), channel_id=1, source_target_pairs={{0,32},{32,0},{64,96},{96,64},{128,160},{160,128},{192,224},{224,1... | collective-permute-start | bytes 208904 | tf_op jit(solution)/shard_map/ppermute | solution.py:223

commit v8 on v7

--- a/solution.py
+++ b/solution.py
@@ -14,7 +14,10 @@
 AHEAD = 2
 PANEL = 16
 LANES = 128
-GROUPS = [[4 * (j % 4) + j // 4 for j in range(16)], [31 - j for j in range(16)]]
+GROUPS = [
+    [4 * (j % 4) + j // 4 for j in range(16)],
+    [16 + 4 * ((j + j // 4) % 4) + j % 4 for j in reversed(range(16))],
+]
 NT = (((1,), (1,)), ((), ()))
 
 

time: 61.9 us -> 61.7 us (level)
    all_to_all x1, blocking collectives: 14.2 us -> 13.5 us  [per_device(): lax.all_to_all(spread, ('core', 'y', 'x'), 0, 0, axis_index_groups=GROUPS)]
where the time goes in v8:
time: 61.7 us; the launch traced here: 61.5 us
  blocking collectives  28.6 us (46%)
  starting transfers between devices  16 us (26%)
  Pallas kernels  8.28 us (13%)
  waiting for transfers between devices  7.97 us (13%)
  between operations  0.67 us (1%)
    all_to_all x1, blocking collectives, per_device(): lax.all_to_all(partial, ('core', 'y', 'x'), 0, 0, axis_index_groups=GROUPS)  15.2 us
    all_to_all x1, blocking collectives, per_device(): lax.all_to_all(spread, ('core', 'y', 'x'), 0, 0, axis_index_groups=GROUPS)  13.5 us
    ppermute x2, starting transfers between devices, swapped(): return lax.ppermute(x, 'z', [p for i, j in swaps for p in ((i, j), (j, i))])  8.44 us
    pallas_call x1, Pallas kernels, per_device(): call(sketch_kernel, 'sketch', (shape((n_col, size, width), F32), pltpu.VM...  4.92 us
    ppermute x2, waiting for transfers between devices, swapped(): return lax.ppermute(x, 'z', [p for i, j in swaps for p in ((i, j), (j, i))])  3.97 us
    ppermute x1, starting transfers between devices, per_device(): total = add(mine, lax.ppermute(other, 'core', swap))  3.72 us
    ppermute x1, starting transfers between devices, per_device(): lax.ppermute(total, ('z', 'core'), [(2 * i + c, 2 * j + 1 - c) for i, j i...  2.49 us
    ppermute x1, waiting for transfers between devices, per_device(): across = lax.ppermute(total, 'z', links)  2.43 us
  transfers between devices with their start and end apart: 6, of which 5 were waited for; matrix products, arithmetic and copies ran while one was open for 0% of the time, Pallas kernels for 0%

profile of v8, /device:TPU:1, one launch (start us, length us, event | category | flops | bytes accessed | tf_op | source)
XLA Modules:
  0.0 61.5 jit_solution(16357745614859699982)
XLA Ops:
  0.6 4.9 %sketch.1 = (f32[16,32,256]{2,1,0:T(8,128)S(1)}, bf16[4096,1024]{1,0:T(8,128)(2,1)S(1)}, f32[8,4096]{1,0:T(8,128)S(1)}) custom-call(bf16[32,1024]{1,0:T(8,128)(2,1)} %sketch_hbm.1, f32[8,4096]{1,0:T(8,128)} %scales_hbm.1, bf16[4096,1024]{1,0:T(8,128)(2,1)} %exposure.1), custom_call_target="tpu_custom_call" | custom-call | tf_op jit(solution)/shard_map/sketch/pallas_call | solution.py:194
  5.6 15.2 %all_to_all.10.x = f32[16,32,256]{2,1,0:T(8,128)S(1)} all-to-all(f32[16,32,256]{2,1,0:T(8,128)S(1)} %get-tuple-element.7), channel_id=1, replica_groups={{0,4,8,12,1,5,9,13,2,6,10,14,3,7,11,15},{27,22,17,28,23,18,29,24,19,30,..., dimensions={0} | all-to-all | bytes 1048576 | tf_op jit(solution)/shard_map/all_to_all | solution.py:203
  20.7 0.1 sum_parts.1
  20.8 13.5 %all_to_all.11.pieces = f32[16,32,256]{2,1,0:T(8,128)S(1)} all-to-all(f32[16,32,256]{2,1,0:T(8,128)S(1)} %sum_parts.1), channel_id=1, replica_groups={{0,4,8,12,1,5,9,13,2,6,10,14,3,7,11,15},{27,22,17,28,23,18,29,24,19,30,..., dimensions={0} | all-to-all | bytes 1048576 | tf_op jit(solution)/shard_map/all_to_all | solution.py:205
  34.3 1.5 %project.1 = (f32[136,128]{1,0:T(8,128)S(1)}, f32[136,128]{1,0:T(8,128)S(1)}) custom-call(f32[16,32,256]{2,1,0:T(8,128)S(1)} %all_to_all.11.pieces, f32[8,4096]{1,0:T(8,128)S(1)} %get-tuple-element.8.scales, bf16[4096,1024]{1,0:T(8,128)(2,1)S(1)} %get-tuple-element.9.exposure), custom_call_target="tpu_custom_call" | custom-call | tf_op jit(solution)/shard_map/project/pallas_call | solution.py:207
  35.8 3.7 %collective-permute-start = (f32[136,128]{1,0:T(8,128)S(1)}, f32[136,128]{1,0:T(8,128)S(1)}, u32[]{:S(2)}, u32[]{:S(2)}) collective-permute-start(f32[136,128]{1,0:T(8,128)S(1)} %get-tuple-element.11), channel_id=1, source_target_pairs={{0,16},{16,0},{1,17},{17,1},{2,18},{18,2},{3,19},{19,3},{4,20},{20... | collective-permute-start | bytes 208904 | tf_op jit(solution)/shard_map/ppermute | solution.py:222
  39.5 0.9 %collective-permute-done.b = f32[136,128]{1,0:T(8,128)S(1)} collective-permute-done((f32[136,128]{1,0:T(8,128)S(1)}, f32[136,128]{1,0:T(8,128)S(1)}, u32[]{:S(2)}, u32[]{:S(2)}) %collective-permute-start) | collective-permute-done | bytes 69664 | tf_op jit(solution)/shard_map/ppermute | solution.py:222
  40.4 4.4 %collective-permute-start.1 = (f32[136,128]{1,0:T(8,128)S(1)}, f32[136,128]{1,0:T(8,128)S(1)}, u32[]{:S(2)}, u32[]{:S(2)}) collective-permute-start(f32[136,128]{1,0:T(8,128)S(1)} %add.3.a), channel_id=1, source_target_pairs={{0,96},{96,0},{32,192},{192,32},{64,160},{160,64},{128,224},{224,1... | collective-permute-start | bytes 208904 | tf_op jit(solution)/shard_map/ppermute | solution.py:220
  44.8 2.3 %collective-permute-done.1.b = f32[136,128]{1,0:T(8,128)S(1)} collective-permute-done((f32[136,128]{1,0:T(8,128)S(1)}, f32[136,128]{1,0:T(8,128)S(1)}, u32[]{:S(2)}, u32[]{:S(2)}) %collective-permute-start.1) | collective-permute-done | bytes 69664 | tf_op jit(solution)/shard_map/ppermute | solution.py:220
  47.1 4.0 %collective-permute-start.2 = (f32[136,128]{1,0:T(8,128)S(1)}, f32[136,128]{1,0:T(8,128)S(1)}, u32[]{:S(2)}, u32[]{:S(2)}) collective-permute-start(f32[136,128]{1,0:T(8,128)S(1)} %add.4.a), channel_id=1, source_target_pairs={{32,64},{64,32},{96,128},{128,96},{160,192},{192,160},{224,0},{0,2... | collective-permute-start | bytes 208904 | tf_op jit(solution)/shard_map/ppermute | solution.py:220
  51.1 1.7 %collective-permute-done.2.b = f32[136,128]{1,0:T(8,128)S(1)} collective-permute-done((f32[136,128]{1,0:T(8,128)S(1)}, f32[136,128]{1,0:T(8,128)S(1)}, u32[]{:S(2)}, u32[]{:S(2)}) %collective-permute-start.2) | collective-permute-done | bytes 69664 | tf_op jit(solution)/shard_map/ppermute | solution.py:220
  52.8 2.5 %collective-permute-start.5 = (f32[136,128]{1,0:T(8,128)S(1)}, f32[136,128]{1,0:T(8,128)S(1)}, u32[]{:S(2)}, u32[]{:S(2)}) collective-permute-start(f32[136,128]{1,0:T(8,128)S(1)} %add.5.mine), channel_id=1, source_target_pairs={{0,48},{16,32},{32,16},{48,0},{64,112},{80,96},{96,80},{112,64},{1... | collective-permute-start | bytes 208904 | tf_op jit(solution)/shard_map/ppermute | solution.py:228
  55.3 0.1 collective-permute-start.4
  55.4 1.3 %collective-permute-start.3 = (f32[136,128]{1,0:T(8,128)S(1)}, f32[136,128]{1,0:T(8,128)S(1)}, u32[]{:S(2)}, u32[]{:S(2)}) collective-permute-start(f32[136,128]{1,0:T(8,128)S(1)} %add.5.mine), channel_id=1, source_target_pairs={{0,32},{32,0},{64,96},{96,64},{128,160},{160,128},{192,224},{224,1... | collective-permute-start | bytes 208904 | tf_op jit(solution)/shard_map/ppermute | solution.py:226
  56.7 0.7 %collective-permute-done.5.corner = f32[136,128]{1,0:T(8,128)S(1)} collective-permute-done((f32[136,128]{1,0:T(8,128)S(1)}, f32[136,128]{1,0:T(8,128)S(1)}, u32[]{:S(2)}, u32[]{:S(2)}) %collective-permute-start.5) | collective-permute-done | bytes 69664 | tf_op jit(solution)/shard_map/ppermute | solution.py:228
  57.3 0.0 collective-permute-done.4.beside
  57.3 2.4 %collective-permute-done.3.across = f32[136,128]{1,0:T(8,128)S(1)} collective-permute-done((f32[136,128]{1,0:T(8,128)S(1)}, f32[136,128]{1,0:T(8,128)S(1)}, u32[]{:S(2)}, u32[]{:S(2)}) %collective-permute-start.3) | collective-permute-done | bytes 69664 | tf_op jit(solution)/shard_map/ppermute | solution.py:226
  59.7 1.8 %solve.1 = (f32[32,4096]{1,0:T(8,128)}, f32[32,1024]{1,0:T(8,128)}) custom-call(f32[136,128]{1,0:T(8,128)S(1)} %add.5.mine, f32[136,128]{1,0:T(8,128)S(1)} %collective-permute-done.3.across, f32[136,128]{1,0:T(8,128)S(1)} %collective-permute-done.4.beside, f32[136,128]{1,0:T(8,128)S(1)} %collective-permute-done.5.corner, f32[16,32,256]{2,1,0:T(8,128)S(1)} %all_to_all.11.pieces), custom_call_target="tpu_custom_call" | custom-call | tf_op jit(solution)/shard_map/solve/pallas_call | solution.py:231
  (3 shorter events, 0.0 us)
Async XLA Ops:
  35.8 4.6 %collective-permute-start = (f32[136,128]{1,0:T(8,128)S(1)}, f32[136,128]{1,0:T(8,128)S(1)}, u32[]{:S(2)}, u32[]{:S(2)}) collective-permute-start(f32[136,128]{1,0:T(8,128)S(1)} %get-tuple-element.11), channel_id=1, source_target_pairs={{0,16},{16,0},{1,17},{17,1},{2,18},{18,2},{3,19},{19,3},{4,20},{20... | collective-permute-start | bytes 208904 | tf_op jit(solution)/shard_map/ppermute | solution.py:222
  40.4 6.7 %collective-permute-start.1 = (f32[136,128]{1,0:T(8,128)S(1)}, f32[136,128]{1,0:T(8,128)S(1)}, u32[]{:S(2)}, u32[]{:S(2)}) collective-permute-start(f32[136,128]{1,0:T(8,128)S(1)} %add.3.a), channel_id=1, source_target_pairs={{0,96},{96,0},{32,192},{192,32},{64,160},{160,64},{128,224},{224,1... | collective-permute-start | bytes 208904 | tf_op jit(solution)/shard_map/ppermute | solution.py:220
  47.1 5.7 %collective-permute-start.2 = (f32[136,128]{1,0:T(8,128)S(1)}, f32[136,128]{1,0:T(8,128)S(1)}, u32[]{:S(2)}, u32[]{:S(2)}) collective-permute-start(f32[136,128]{1,0:T(8,128)S(1)} %add.4.a), channel_id=1, source_target_pairs={{32,64},{64,32},{96,128},{128,96},{160,192},{192,160},{224,0},{0,2... | collective-permute-start | bytes 208904 | tf_op jit(solution)/shard_map/ppermute | solution.py:220
  52.8 4.5 %collective-permute-start.5 = (f32[136,128]{1,0:T(8,128)S(1)}, f32[136,128]{1,0:T(8,128)S(1)}, u32[]{:S(2)}, u32[]{:S(2)}) collective-permute-start(f32[136,128]{1,0:T(8,128)S(1)} %add.5.mine), channel_id=1, source_target_pairs={{0,48},{16,32},{32,16},{48,0},{64,112},{80,96},{96,80},{112,64},{1... | collective-permute-start | bytes 208904 | tf_op jit(solution)/shard_map/ppermute | solution.py:228
  55.3 2.0 %collective-permute-start.4 = (f32[136,128]{1,0:T(8,128)S(1)}, f32[136,128]{1,0:T(8,128)S(1)}, u32[]{:S(2)}, u32[]{:S(2)}) collective-permute-start(f32[136,128]{1,0:T(8,128)S(1)} %add.5.mine), channel_id=1, source_target_pairs={{0,16},{16,0},{1,17},{17,1},{2,18},{18,2},{3,19},{19,3},{4,20},{20... | collective-permute-start | bytes 208904 | tf_op jit(solution)/shard_map/ppermute | solution.py:227
  55.4 4.4 %collective-permute-start.3 = (f32[136,128]{1,0:T(8,128)S(1)}, f32[136,128]{1,0:T(8,128)S(1)}, u32[]{:S(2)}, u32[]{:S(2)}) collective-permute-start(f32[136,128]{1,0:T(8,128)S(1)} %add.5.mine), channel_id=1, source_target_pairs={{0,32},{32,0},{64,96},{96,64},{128,160},{160,128},{192,224},{224,1... | collective-permute-start | bytes 208904 | tf_op jit(solution)/shard_map/ppermute | solution.py:226

commit v9 on v4

--- a/solution.py
+++ b/solution.py
@@ -18,8 +18,12 @@
 }
 ORDER = "cba"
 AHEAD = 2
-PANEL = 8
+PANEL = 16
 LANES = 128
+GROUPS = [
+    [4 * (j % 4) + j // 4 for j in range(16)],
+    [16 + 4 * ((j + j // 4) % 4) + j % 4 for j in reversed(range(16))],
+]
 NT = (((1,), (1,)), ((), ()))
 
 
@@ -32,7 +36,7 @@
     return slice(b * LANES, (b + n) * LANES)
 
 
-def sketch_kernel(sketch_hbm, scales_hbm, exposure, out, held, sketch, scales, diag, sems, small):
+def sketch_kernel(sketch_hbm, scales_hbm, exposure, out, held, scales, sketch, diag, sems, small):
     size = sketch.shape[0]
     blocks = scales.shape[0]
     groups, _, width = out.shape
@@ -73,8 +77,11 @@
         out[j] = total
 
 
-def add_kernel(a, b, out):
-    out[...] = a[...] + b[...]
+def add_kernel(*refs):
+    parts = [r[...] for r in refs[:-1]]
+    while len(parts) > 1:
+        parts = [parts[i] + parts[i + 1] for i in range(0, len(parts), 2)]
+    refs[-1][...] = parts[0]
 
 
 def project_kernel(pieces, scales, exposure, mine, other, both, w, acc):
@@ -195,17 +202,18 @@
     shape = jax.ShapeDtypeStruct
     DMA = pltpu.SemaphoreType.DMA
 
-    partial, held = call(
-        sketch_kernel, "sketch", (shape((n_col, size, width), F32), pltpu.VMEM((rows, cols), BF)),
+    partial, held, scales = call(
+        sketch_kernel, "sketch",
+        (shape((n_col, size, width), F32), pltpu.VMEM((rows, cols), BF), pltpu.VMEM((blocks, rows), F32)),
         [HBM] * 3, 40,
         [
-            pltpu.VMEM((size, cols), BF), pltpu.VMEM((blocks, rows), F32),
+            pltpu.VMEM((size, cols), BF),
             pltpu.VMEM((blocks * size, cols), BF), DMA((CHUNKS,)), DMA((2,)),
         ],
     )(*(pltpu.with_memory_space_constraint(x, pltpu.HBM) for x in (sketch, scales, exposure)))
-    got = lax.all_to_all(partial, ("y", "x"), 0, 0)
+    got = lax.all_to_all(partial, ("core", "y", "x"), 0, 0, axis_index_groups=GROUPS)
     spread = call(sum_copies_kernel, "sum_parts", shape((n_col, size, width), F32), [VM])(got)
-    pieces = lax.all_to_all(spread, ("y", "x"), 0, 0)
+    pieces = lax.all_to_all(spread, ("core", "y", "x"), 0, 0, axis_index_groups=GROUPS)
 
     mine, other = call(
         project_kernel, "project", (shape((tall, LANES), F32),) * 2, [VM, VM, VM], 40,
@@ -215,11 +223,22 @@
         ],
     )(pieces, scales, held)
 
-    add = call(add_kernel, "add", shape((tall, LANES), F32), [VM, VM])
+    def add(*xs):
+        return call(add_kernel, "add", shape((tall, LANES), F32), [VM] * len(xs))(*xs)
+
+    def pairs(x, swaps):
+        return add(x, lax.ppermute(x, "z", [p for i, j in swaps for p in ((i, j), (j, i))]))
+
+    def quad(x, moves):
+        return add(x, *(lax.ppermute(x, "z", [(i, f(i)) for i in range(n_z)]) for f in moves))
+
     total = add(mine, lax.ppermute(other, "core", swap))
-    for step in ORDER:
-        both_ways = [p for i, j in PAIRS[step] for p in ((i, j), (j, i))]
-        total = add(total, lax.ppermute(total, "z", both_ways))
+    total = pairs(total, ((0, 1), (2, 3), (4, 5), (6, 7)))
+    total = add(
+        total, lax.ppermute(total, "z", [p for i, j in ((0, 3), (1, 2), (4, 7), (5, 6)) for p in ((i, j), (j, i))]),
+        lax.ppermute(total, "z", [p for i, j in ((0, 7), (3, 4), (1, 6), (2, 5)) for p in ((i, j), (j, i))]),
+        lax.ppermute(total, "z", [p for i, j in ((0, 5), (1, 4), (2, 7), (3, 6)) for p in ((i, j), (j, i))]),
+    )
     total_other = lax.ppermute(total, "core", swap)
     lower, basis = call(
         functools.partial(solve_kernel, float(total_paths) ** 0.5), "solve",

time: 64.3 us -> 61.8 us (0.961)
  blocking collectives: 31 us -> 28.6 us
  starting transfers between devices: 15.2 us -> 16.3 us
  waiting for transfers between devices: 7.63 us -> 6.86 us
    all_to_all x2, blocking collectives: 31 us -> 28.6 us  [the longest x1 15.2 us: per_device(): lax.all_to_all(partial, ('core', 'y', 'x'), 0, 0, axis_index_groups=GROUPS)]
    ppermute x1, starting transfers between devices: 2.66 us -> 3.72 us  [per_device(): total = add(mine, lax.ppermute(other, 'core', swap))]
    ppermute x3 -> x4, waiting for transfers between devices: 6.72 us -> 5.95 us  [the longest x1 2.57 us: per_device(): lax.ppermute(total, 'z', [p for i, j in ((0, 7), (3, 4), (1, 6), (2, 5))...]
    ppermute x3 -> x4, starting transfers between devices: 8.93 us -> 9.28 us  [the longest x1 5.9 us: per_device(): lax.ppermute(total, 'z', [p for i, j in ((0, 5), (1, 4), (2, 7), (3, 6))...]
  transfers between devices with their start and end apart: 5 -> 6, of which waited for: 4 -> 5; matrix products, arithmetic and copies ran while one was open for 0% -> 0% of each run, Pallas kernels for 3% -> 3%
where the time goes in v9:
time: 61.8 us; the launch traced here: 61.6 us
  blocking collectives  28.6 us (46%)
  starting transfers between devices  16.3 us (26%)
  Pallas kernels  9.13 us (15%)
  waiting for transfers between devices  6.86 us (11%)
  between operations  0.67 us (1%)
    all_to_all x1, blocking collectives, per_device(): lax.all_to_all(partial, ('core', 'y', 'x'), 0, 0, axis_index_groups=GROUPS)  15.2 us
    all_to_all x1, blocking collectives, per_device(): lax.all_to_all(spread, ('core', 'y', 'x'), 0, 0, axis_index_groups=GROUPS)  13.5 us
    ppermute x1, starting transfers between devices, per_device(): lax.ppermute(total, 'z', [p for i, j in ((0, 5), (1, 4), (2, 7), (3, 6))...  5.9 us
    pallas_call x1, Pallas kernels, per_device(): call(sketch_kernel, 'sketch', (shape((n_col, size, width), F32), pltpu.VM...  4.92 us
    ppermute x1, starting transfers between devices, per_device(): total = add(mine, lax.ppermute(other, 'core', swap))  3.72 us
    ppermute x1, starting transfers between devices, per_device(): total_other = lax.ppermute(total, 'core', swap)  3.29 us
    ppermute x1, waiting for transfers between devices, per_device(): lax.ppermute(total, 'z', [p for i, j in ((0, 7), (3, 4), (1, 6), (2, 5))...  2.57 us
    ppermute x1, waiting for transfers between devices, pairs(): lax.ppermute(x, 'z', [p for i, j in swaps for p in ((i, j), (j, i))])  2.16 us
  transfers between devices with their start and end apart: 6, of which 5 were waited for; matrix products, arithmetic and copies ran while one was open for 0% of the time, Pallas kernels for 3%

profile of v9, /device:TPU:1, one launch (start us, length us, event | category | flops | bytes accessed | tf_op | source)
XLA Modules:
  0.0 61.6 jit_solution(8713847902875231283)
XLA Ops:
  0.6 4.9 %sketch.1 = (f32[16,32,256]{2,1,0:T(8,128)S(1)}, bf16[4096,1024]{1,0:T(8,128)(2,1)S(1)}, f32[8,4096]{1,0:T(8,128)S(1)}) custom-call(bf16[32,1024]{1,0:T(8,128)(2,1)} %sketch_hbm.1, f32[8,4096]{1,0:T(8,128)} %scales_hbm.1, bf16[4096,1024]{1,0:T(8,128)(2,1)} %exposure.1), custom_call_target="tpu_custom_call" | custom-call | tf_op jit(solution)/shard_map/sketch/pallas_call | solution.py:205
  5.6 15.2 %all_to_all.10.x = f32[16,32,256]{2,1,0:T(8,128)S(1)} all-to-all(f32[16,32,256]{2,1,0:T(8,128)S(1)} %get-tuple-element.9), channel_id=1, replica_groups={{0,4,8,12,1,5,9,13,2,6,10,14,3,7,11,15},{27,22,17,28,23,18,29,24,19,30,..., dimensions={0} | all-to-all | bytes 1048576 | tf_op jit(solution)/shard_map/all_to_all | solution.py:214
  20.7 0.1 sum_parts.1
  20.8 13.5 %all_to_all.11.pieces = f32[16,32,256]{2,1,0:T(8,128)S(1)} all-to-all(f32[16,32,256]{2,1,0:T(8,128)S(1)} %sum_parts.1), channel_id=1, replica_groups={{0,4,8,12,1,5,9,13,2,6,10,14,3,7,11,15},{27,22,17,28,23,18,29,24,19,30,..., dimensions={0} | all-to-all | bytes 1048576 | tf_op jit(solution)/shard_map/all_to_all | solution.py:216
  34.3 1.5 %project.1 = (f32[136,128]{1,0:T(8,128)S(1)}, f32[136,128]{1,0:T(8,128)S(1)}) custom-call(f32[16,32,256]{2,1,0:T(8,128)S(1)} %all_to_all.11.pieces, f32[8,4096]{1,0:T(8,128)S(1)} %get-tuple-element.10.scales, bf16[4096,1024]{1,0:T(8,128)(2,1)S(1)} %get-tuple-element.11.exposure), custom_call_target="tpu_custom_call" | custom-call | tf_op jit(solution)/shard_map/project/pallas_call | solution.py:218
  35.8 3.7 %collective-permute-start = (f32[136,128]{1,0:T(8,128)S(1)}, f32[136,128]{1,0:T(8,128)S(1)}, u32[]{:S(2)}, u32[]{:S(2)}) collective-permute-start(f32[136,128]{1,0:T(8,128)S(1)} %get-tuple-element.13), channel_id=1, source_target_pairs={{0,16},{16,0},{1,17},{17,1},{2,18},{18,2},{3,19},{19,3},{4,20},{20... | collective-permute-start | bytes 208904 | tf_op jit(solution)/shard_map/ppermute | solution.py:235
  39.5 0.9 %collective-permute-done.refs_1_ = f32[136,128]{1,0:T(8,128)S(1)} collective-permute-done((f32[136,128]{1,0:T(8,128)S(1)}, f32[136,128]{1,0:T(8,128)S(1)}, u32[]{:S(2)}, u32[]{:S(2)}) %collective-permute-start) | collective-permute-done | bytes 69664 | tf_op jit(solution)/shard_map/ppermute | solution.py:235
  40.4 1.7 %collective-permute-start.1 = (f32[136,128]{1,0:T(8,128)S(1)}, f32[136,128]{1,0:T(8,128)S(1)}, u32[]{:S(2)}, u32[]{:S(2)}) collective-permute-start(f32[136,128]{1,0:T(8,128)S(1)} %add.3.refs_0_), channel_id=1, source_target_pairs={{0,32},{32,0},{64,96},{96,64},{128,160},{160,128},{192,224},{224,1... | collective-permute-start | bytes 208904 | tf_op jit(solution)/shard_map/ppermute | solution.py:230
  42.1 2.2 %collective-permute-done.1.refs_1_ = f32[136,128]{1,0:T(8,128)S(1)} collective-permute-done((f32[136,128]{1,0:T(8,128)S(1)}, f32[136,128]{1,0:T(8,128)S(1)}, u32[]{:S(2)}, u32[]{:S(2)}) %collective-permute-start.1) | collective-permute-done | bytes 69664 | tf_op jit(solution)/shard_map/ppermute | solution.py:230
  44.3 5.9 %collective-permute-start.4 = (f32[136,128]{1,0:T(8,128)S(1)}, f32[136,128]{1,0:T(8,128)S(1)}, u32[]{:S(2)}, u32[]{:S(2)}) collective-permute-start(f32[136,128]{1,0:T(8,128)S(1)} %add.4.refs_0_), channel_id=1, source_target_pairs={{0,160},{160,0},{32,128},{128,32},{64,224},{224,64},{96,192},{192,... | collective-permute-start | bytes 208904 | tf_op jit(solution)/shard_map/ppermute | solution.py:240
  50.2 0.0 collective-permute-start.3
  50.2 1.6 %collective-permute-start.2 = (f32[136,128]{1,0:T(8,128)S(1)}, f32[136,128]{1,0:T(8,128)S(1)}, u32[]{:S(2)}, u32[]{:S(2)}) collective-permute-start(f32[136,128]{1,0:T(8,128)S(1)} %add.4.refs_0_), channel_id=1, source_target_pairs={{0,96},{96,0},{32,64},{64,32},{128,224},{224,128},{160,192},{192,1... | collective-permute-start | bytes 208904 | tf_op jit(solution)/shard_map/ppermute | solution.py:238
  51.9 0.2 collective-permute-done.4.refs_3_
  52.0 2.6 %collective-permute-done.3.refs_2_ = f32[136,128]{1,0:T(8,128)S(1)} collective-permute-done((f32[136,128]{1,0:T(8,128)S(1)}, f32[136,128]{1,0:T(8,128)S(1)}, u32[]{:S(2)}, u32[]{:S(2)}) %collective-permute-start.3) | collective-permute-done | bytes 69664 | tf_op jit(solution)/shard_map/ppermute | solution.py:239
  54.6 1.1 %collective-permute-done.2.refs_1_ = f32[136,128]{1,0:T(8,128)S(1)} collective-permute-done((f32[136,128]{1,0:T(8,128)S(1)}, f32[136,128]{1,0:T(8,128)S(1)}, u32[]{:S(2)}, u32[]{:S(2)}) %collective-permute-start.2) | collective-permute-done | bytes 69664 | tf_op jit(solution)/shard_map/ppermute | solution.py:238
  55.7 3.3 %collective-permute-start.5 = (f32[136,128]{1,0:T(8,128)S(1)}, f32[136,128]{1,0:T(8,128)S(1)}, u32[]{:S(2)}, u32[]{:S(2)}) collective-permute-start(f32[136,128]{1,0:T(8,128)S(1)} %add.5.x.mine), channel_id=1, source_target_pairs={{0,16},{16,0},{1,17},{17,1},{2,18},{18,2},{3,19},{19,3},{4,20},{20... | collective-permute-start | bytes 208904 | tf_op jit(solution)/shard_map/ppermute | solution.py:242
  59.0 1.8 %solve.1 = (f32[32,32]{1,0:T(8,128)S(1)}, f32[32,4096]{1,0:T(8,128)}) custom-call(f32[136,128]{1,0:T(8,128)S(1)} %add.5.x.mine, f32[16,32,256]{2,1,0:T(8,128)S(1)} %all_to_all.11.pieces), custom_call_target="tpu_custom_call" | custom-call | tf_op jit(solution)/shard_map/solve/pallas_call | solution.py:243
  60.7 0.0 collective-permute-done.5.other
  60.7 0.9 %finish.1 = f32[32,1024]{1,0:T(8,128)} custom-call(f32[32,32]{1,0:T(8,128)S(1)} %get-tuple-element.15.lower, f32[136,128]{1,0:T(8,128)S(1)} %add.5.x.mine, f32[136,128]{1,0:T(8,128)S(1)} %collective-permute-done.5.other), custom_call_target="tpu_custom_call" | custom-call | tf_op jit(solution)/shard_map/finish/pallas_call | solution.py:247
  (3 shorter events, 0.0 us)
Async XLA Ops:
  35.8 4.6 %collective-permute-start = (f32[136,128]{1,0:T(8,128)S(1)}, f32[136,128]{1,0:T(8,128)S(1)}, u32[]{:S(2)}, u32[]{:S(2)}) collective-permute-start(f32[136,128]{1,0:T(8,128)S(1)} %get-tuple-element.13), channel_id=1, source_target_pairs={{0,16},{16,0},{1,17},{17,1},{2,18},{18,2},{3,19},{19,3},{4,20},{20... | collective-permute-start | bytes 208904 | tf_op jit(solution)/shard_map/ppermute | solution.py:235
  40.4 3.9 %collective-permute-start.1 = (f32[136,128]{1,0:T(8,128)S(1)}, f32[136,128]{1,0:T(8,128)S(1)}, u32[]{:S(2)}, u32[]{:S(2)}) collective-permute-start(f32[136,128]{1,0:T(8,128)S(1)} %add.3.refs_0_), channel_id=1, source_target_pairs={{0,32},{32,0},{64,96},{96,64},{128,160},{160,128},{192,224},{224,1... | collective-permute-start | bytes 208904 | tf_op jit(solution)/shard_map/ppermute | solution.py:230
  44.3 7.7 %collective-permute-start.4 = (f32[136,128]{1,0:T(8,128)S(1)}, f32[136,128]{1,0:T(8,128)S(1)}, u32[]{:S(2)}, u32[]{:S(2)}) collective-permute-start(f32[136,128]{1,0:T(8,128)S(1)} %add.4.refs_0_), channel_id=1, source_target_pairs={{0,160},{160,0},{32,128},{128,32},{64,224},{224,64},{96,192},{192,... | collective-permute-start | bytes 208904 | tf_op jit(solution)/shard_map/ppermute | solution.py:240
  50.2 4.4 %collective-permute-start.3 = (f32[136,128]{1,0:T(8,128)S(1)}, f32[136,128]{1,0:T(8,128)S(1)}, u32[]{:S(2)}, u32[]{:S(2)}) collective-permute-start(f32[136,128]{1,0:T(8,128)S(1)} %add.4.refs_0_), channel_id=1, source_target_pairs={{0,224},{224,0},{96,128},{128,96},{32,192},{192,32},{64,160},{160,... | collective-permute-start | bytes 208904 | tf_op jit(solution)/shard_map/ppermute | solution.py:239
  50.2 5.4 %collective-permute-start.2 = (f32[136,128]{1,0:T(8,128)S(1)}, f32[136,128]{1,0:T(8,128)S(1)}, u32[]{:S(2)}, u32[]{:S(2)}) collective-permute-start(f32[136,128]{1,0:T(8,128)S(1)} %add.4.refs_0_), channel_id=1, source_target_pairs={{0,96},{96,0},{32,64},{64,32},{128,224},{224,128},{160,192},{192,1... | collective-permute-start | bytes 208904 | tf_op jit(solution)/shard_map/ppermute | solution.py:238
  55.7 5.1 %collective-permute-start.5 = (f32[136,128]{1,0:T(8,128)S(1)}, f32[136,128]{1,0:T(8,128)S(1)}, u32[]{:S(2)}, u32[]{:S(2)}) collective-permute-start(f32[136,128]{1,0:T(8,128)S(1)} %add.5.x.mine), channel_id=1, source_target_pairs={{0,16},{16,0},{1,17},{17,1},{2,18},{18,2},{3,19},{19,3},{4,20},{20... | collective-permute-start | bytes 208904 | tf_op jit(solution)/shard_map/ppermute | solution.py:242
